TPU v7x, 32 devices: a whole 2x2x4 slice. The times are simulated.
32 devices in a mesh: mod: 2 (over core), batch: 16 (over z, y, x).
Axes of the slice: x: 2, y: 2, z: 4, core: 2. Of those that a mesh axis runs over, the one named last changes fastest.
Arguments:
- speech_feats: bfloat16 [2, 8192, 512], P(None, 'batch'), may hold values from -6 to 6
- text_ids: int32 [2, 8192], P(None, 'batch'), may hold values from 0 to 80
- routes: int32 [2, 16, 2, 2], P(None, 'batch'), may hold values from 0 to 7, as said below
- lengths: int32 [2, 16, 2, 2], P(None, 'batch'), may hold values from 64 to 128
- buckets: int32 [511], replicated, may hold values from 0 to 159
- post_cot: bfloat16 [2, 2, 8192, 81], P('mod', None, 'batch'), may hold values from -6 to 6
- ln1_gain: bfloat16 [768], replicated, may hold values from 0.5 to 1.5
- ln1_bias: bfloat16 [768], replicated, may hold values from -1.75 to 1.75
- w_qkv: bfloat16 [768, 2304], replicated, may hold values from -0.21875 to 0.21875
- bias_qv: bfloat16 [2, 768], replicated, may hold values from -1.75 to 1.75
- rel_table: bfloat16 [160, 12], replicated, may hold values from -6 to 6
- w_attn_out: bfloat16 [768, 768], replicated, may hold values from -0.625 to 0.625
- bias_attn_out: bfloat16 [768], replicated, may hold values from -1.75 to 1.75
- ln2_gain: bfloat16 [768], replicated, may hold values from 0.5 to 1.5
- ln2_bias: bfloat16 [768], replicated, may hold values from -1.75 to 1.75
- w_ffn_in: bfloat16 [768, 3072], replicated, may hold values from -0.21875 to 0.21875
- bias_ffn_in: bfloat16 [3072], replicated, may hold values from -1.75 to 1.75
- w_ffn_out: bfloat16 [3072, 768], replicated, may hold values from -0.109375 to 0.109375
- bias_ffn_out: bfloat16 [768], replicated, may hold values from -1.75 to 1.75
- speech_proj: bfloat16 [512, 768], replicated, may hold values from -0.25 to 0.25
- speech_bias: bfloat16 [768], replicated, may hold values from -1.75 to 1.75
- text_table: bfloat16 [81, 768], replicated, may hold values from -6 to 6
- post_weight: bfloat16 [2, 768, 81], replicated, may hold values from -0.625 to 0.625
Outputs:
- encoded: bfloat16 [2, 8192, 768], P(None, ('mod', 'batch'))
- embed_grad: bfloat16 [2, 8192, 768], P(None, ('mod', 'batch'))
- grad_ln1_gain: float32 [768], replicated
- grad_ln1_bias: float32 [768], replicated
- grad_w_qkv: float32 [768, 2304], replicated
- grad_bias_qv: float32 [2, 768], replicated
- grad_rel_table: float32 [160, 12], replicated
- grad_w_attn_out: float32 [768, 768], replicated
- grad_bias_attn_out: float32 [768], replicated
- grad_ln2_gain: float32 [768], replicated
- grad_ln2_bias: float32 [768], replicated
- grad_w_ffn_in: float32 [768, 3072], replicated
- grad_bias_ffn_in: float32 [3072], replicated
- grad_w_ffn_out: float32 [3072, 768], replicated
- grad_bias_ffn_out: float32 [768], replicated
- grad_speech_proj: float32 [512, 768], replicated
- grad_speech_bias: float32 [768], replicated
- grad_text_table: float32 [81, 768], replicated
- grad_post_weight: float32 [2, 768, 81], replicated
Inputs may be any that keep to these rules, and one draw needn't show every extreme that they name: routes[m, b, d, j] is 4 times a modality (0 speech, 1 text) plus a source block index; the 2 slots of one device in one micro-batch name one modality, and the slots of the two devices of one batch index name distinct source blocks.
All inputs are finite; a program needn't handle non-finite values.
Results may differ from a plain program's by a relative error of at most 0.012.
Values may be sent and summed in bfloat16 or wider, within the bound.
No kernel may reach another device: no remote copies, remote signals or barrier semaphores. Data moves between devices by JAX's collectives and lax.ppermute only.
A program may use at most 192 MiB of HBM per device.

v0:
```python
import functools

import jax
import jax.numpy as jnp
from jax import lax
from jax.experimental import pallas as pl
from jax.experimental.pallas import tpu as pltpu
from jax.sharding import PartitionSpec as P

F32 = jnp.float32
BF16 = jnp.bfloat16
HEADS = 12
HEAD_DIM = 64
SEQ = 256
ROWS = 128
MICRO = 2
SRC = 4
D = 768
FF = 3072
OUT = 81
EPSILON = 1e-05
NEGATIVE = -1e30
VMEM_LIMIT = 56 * 1024 * 1024
AXES = ("mod", "batch")

G1, S1, BQ, BV, BAO, G2, S2, BFO, SB, BFI = range(10)
SMALL_ROWS = 32
REL_ROW = 16


def dot(a, b):
    return lax.dot_general(a, b, (((1,), (0,)), ((), ())), preferred_element_type=F32)


def dot_nt(a, b):
    return lax.dot_general(a, b, (((1,), (1,)), ((), ())), preferred_element_type=F32)


def dot_tn(a, b):
    return lax.dot_general(a, b, (((0,), (0,)), ((), ())), preferred_element_type=F32)


def iota(shape, axis):
    return lax.broadcasted_iota(jnp.int32, shape, axis)


def aligned(start, size):
    return pl.ds(pl.multiple_of(start, size), size)


def normalise(values):
    centred = values - jnp.mean(values, axis=-1, keepdims=True)
    inverse = lax.rsqrt(jnp.mean(centred * centred, axis=-1, keepdims=True) + EPSILON)
    return centred * inverse, inverse


def norm_back(grad, normed, inverse, gain):
    scaled = grad * gain
    mean_grad = jnp.mean(scaled, axis=-1, keepdims=True)
    along = jnp.mean(scaled * normed, axis=-1, keepdims=True)
    return inverse * (scaled - mean_grad - normed * along)


def head_masks():
    lane = iota((1, 2 * HEAD_DIM), 1)
    low = (lane < HEAD_DIM).astype(F32).astype(BF16)
    return low, (1.0 - low.astype(F32)).astype(BF16)


def route_of(routes_ref, d, m, j):
    route = routes_ref[m * 4 + d * 2 + j]
    return route // SRC, route % SRC


def onehot_vocab(ids_ref, m, block):
    row_ids = ids_ref[m : m + 1, aligned(block * ROWS, ROWS)]
    return (iota((ROWS, ROWS), 0) == row_ids).astype(F32).astype(BF16)


def front_kernel(
    d_ref, routes_ref, lengths_ref,
    feats_ref, ids_ref, bucket_ref, rel_ref, proj_ref, table_ref, vec_ref, wqkv_hbm, wao_hbm,
    x_ref, h1_ref, qkv_ref, pt_ref, ctx_ref, mid_ref, h2_ref,
    wqkv, wao, sems, bias, mask, frow, tab,
):
    d = d_ref[0]
    copy_qkv = pltpu.make_async_copy(wqkv_hbm, wqkv, sems.at[0])
    copy_ao = pltpu.make_async_copy(wao_hbm, wao, sems.at[1])
    copy_qkv.start()
    copy_ao.start()
    vocab = table_ref.shape[0]
    tab[...] = jnp.zeros_like(tab)
    tab[:vocab, :] = table_ref[...]
    for m in range(MICRO):
        for j in range(2):
            modality, block = route_of(routes_ref, d, m, j)
            rows = slice((m * 2 + j) * ROWS, (m * 2 + j + 1) * ROWS)

            @pl.when(modality == 0)
            def _(m=m, block=block, rows=rows):
                feats = feats_ref[m, aligned(block * ROWS, ROWS), :]
                spoken = dot(feats, proj_ref[...]) + vec_ref[SB : SB + 1, :]
                x_ref[rows, :] = spoken.astype(BF16)

            @pl.when(modality != 0)
            def _(m=m, block=block, rows=rows):
                hot = onehot_vocab(ids_ref, m, block)
                x_ref[rows, :] = dot_tn(hot, tab[...]).astype(BF16)

    hot = (iota((rel_ref.shape[1], 2 * SEQ), 0) == bucket_ref[...]).astype(F32).astype(BF16)
    frow[...] = dot(rel_ref[...], hot)

    def make_bias(h, _):
        base = jnp.broadcast_to(frow[pl.ds(h, 1), :], (16, 2 * SEQ))
        base = pltpu.roll(base, 0, 1, stride=1, stride_axis=0)
        for a in range(SEQ // 16):
            shifted = pltpu.roll(base, 16 * a, 1) if a else base
            bias[h, 16 * a : 16 * a + 16, :] = shifted[:, :SEQ].astype(BF16)
        return 0

    lax.fori_loop(0, HEADS, make_bias, 0)
    at_j = iota((SEQ, SEQ), 0)
    at_i = iota((SEQ, SEQ), 1)
    for m in range(MICRO):
        modality, _ = route_of(routes_ref, d, m, 0)
        first = lengths_ref[m * 4 + d * 2]
        second = lengths_ref[m * 4 + d * 2 + 1]
        whole = jnp.where(at_j < first + second, 0.0, NEGATIVE)
        limit = jnp.where(at_j < ROWS, first, second + ROWS)
        same = (at_j // ROWS) == (at_i // ROWS)
        halves = jnp.where(same, jnp.where(at_j < limit, 0.0, NEGATIVE), NEGATIVE)
        mask[m] = jnp.where(modality == 0, whole, halves)

    def first_norm(r, _):
        rows = aligned(r * ROWS, ROWS)
        normed, _ = normalise(x_ref[rows, :].astype(F32))
        h1_ref[rows, :] = (normed * vec_ref[G1 : G1 + 1, :] + vec_ref[S1 : S1 + 1, :]).astype(BF16)
        return 0

    lax.fori_loop(0, MICRO * SEQ // ROWS, first_norm, 0)
    copy_qkv.wait()
    for n in range(9):
        cols = slice(n * 256, (n + 1) * 256)
        part = dot(h1_ref[...], wqkv[:, cols])
        if n < 3:
            part = part + vec_ref[BQ : BQ + 1, cols]
        elif n >= 6:
            part = part + vec_ref[BV : BV + 1, (n - 6) * 256 : (n - 5) * 256]
        qkv_ref[:, cols] = part.astype(BF16)

    low, high = head_masks()

    def attention(step, _):
        m = step // (HEADS // 2)
        pair = step - m * (HEADS // 2)
        rows = aligned(m * SEQ, SEQ)
        q = qkv_ref[rows, aligned(pair * 128, 128)]
        k = qkv_ref[rows, aligned(D + pair * 128, 128)]
        v = qkv_ref[rows, aligned(2 * D + pair * 128, 128)]
        total = jnp.zeros((SEQ, 128), F32)
        for s, keep in enumerate((low, high)):
            scores = dot_nt(k * keep, q) * HEAD_DIM ** (-0.5)
            scores = scores + bias[2 * pair + s].astype(F32) + mask[m]
            weights = jnp.exp(scores - jnp.max(scores, axis=0, keepdims=True))
            weights = weights * (1.0 / jnp.sum(weights, axis=0, keepdims=True))
            weights = weights.astype(BF16)
            pt_ref[m * HEADS + 2 * pair + s] = weights
            total = total + dot_tn(weights, v * keep)
        ctx_ref[rows, aligned(pair * 128, 128)] = total.astype(BF16)
        return 0

    lax.fori_loop(0, MICRO * HEADS // 2, attention, 0)
    copy_ao.wait()
    for n in range(3):
        cols = slice(n * 256, (n + 1) * 256)
        mid_ref[:, cols] = (
            x_ref[:, cols].astype(F32) + dot(ctx_ref[...], wao[:, cols]) + vec_ref[BAO : BAO + 1, cols]
        )

    def second_norm(r, _):
        rows = aligned(r * ROWS, ROWS)
        normed, _ = normalise(mid_ref[rows, :])
        h2_ref[rows, :] = (normed * vec_ref[G2 : G2 + 1, :] + vec_ref[S2 : S2 + 1, :]).astype(BF16)
        return 0

    lax.fori_loop(0, MICRO * SEQ // ROWS, second_norm, 0)


def smem():
    return pl.BlockSpec(memory_space=pltpu.SMEM)


def vmem():
    return pl.BlockSpec(memory_space=pltpu.VMEM)


def params(semantics=None):
    return pltpu.CompilerParams(vmem_limit_bytes=VMEM_LIMIT, dimension_semantics=semantics)


def front(d, routes, lengths, feats, ids, bucket_row, rel, proj, table, vecs, w_qkv, w_ao):
    rows = MICRO * SEQ
    shapes = [
        jax.ShapeDtypeStruct((rows, D), BF16),
        jax.ShapeDtypeStruct((rows, D), BF16),
        jax.ShapeDtypeStruct((rows, 3 * D), BF16),
        jax.ShapeDtypeStruct((MICRO * HEADS, SEQ, SEQ), BF16),
        jax.ShapeDtypeStruct((rows, D), BF16),
        jax.ShapeDtypeStruct((rows, D), F32),
        jax.ShapeDtypeStruct((rows, D), BF16),
    ]
    return pl.pallas_call(
        front_kernel,
        out_shape=shapes,
        in_specs=[smem()] * 3 + [vmem()] * 7 + [pl.BlockSpec(memory_space=pl.ANY)] * 2,
        out_specs=[vmem()] * 7,
        scratch_shapes=[
            pltpu.VMEM((D, 3 * D), BF16),
            pltpu.VMEM((D, D), BF16),
            pltpu.SemaphoreType.DMA((2,)),
            pltpu.VMEM((HEADS, SEQ, SEQ), BF16),
            pltpu.VMEM((MICRO, SEQ, SEQ), F32),
            pltpu.VMEM((16, 2 * SEQ), F32),
            pltpu.VMEM((ROWS, D), BF16),
        ],
        compiler_params=params(),
        cost_estimate=pl.CostEstimate(flops=4_000_000_000, bytes_accessed=20_000_000, transcendentals=1_600_000),
        name="front",
    )(d, routes, lengths, feats, ids, bucket_row, rel, proj, table, vecs, w_qkv, w_ao)


def gelu_parts(before):
    cdf = 0.5 * (1.0 + lax.erf(before * 0.7071067811865476))
    pdf = jnp.exp(before * before * -0.5) * 0.3989422804014327
    return before * cdf, cdf + before * pdf


CHUNK = 768


def ffn_chunk(h2_ref, ge, win_ref, wout_ref, bias_row, act, gb, h2t, dwout_ref, dwin_ref, dbin_ref):
    for n in range(CHUNK // 256):
        cols = slice(n * 256, (n + 1) * 256)
        before = dot(h2_ref[...], win_ref[:, cols]) + bias_row[:, cols]
        grad = dot_nt(ge[...], wout_ref[cols, :])
        value, slope = gelu_parts(before)
        act[:, cols] = value.astype(BF16)
        low = (grad * slope).astype(BF16)
        gb[:, cols] = low
        dbin_ref[0, :, cols] = jnp.sum(low.astype(F32), axis=0, keepdims=True)
    for n in range(CHUNK // 256):
        cols = slice(n * 256, (n + 1) * 256)
        dwout_ref[cols, :] = dot_tn(act[:, cols], ge[...]).astype(BF16)
        dwin_ref[:, cols] = dot(h2t[...], gb[:, cols]).astype(BF16)


def ffn_first_kernel(
    half_ref, d_ref, routes_ref, lengths_ref,
    h2_ref, mid_ref, vec_ref, cot_mine, cot_other, post_ref, win_ref, wout_ref,
    enc_ref, gh_ref, ge_ref, cot_ref, dwout_ref, dwin_ref, dbin_ref,
    act, gb, h2t,
):
    step = pl.program_id(0)

    @pl.when(step == 0)
    def _():
        d = d_ref[0]
        h2t[...] = jnp.transpose(h2_ref[...])
        for m in range(MICRO):
            first = lengths_ref[m * 4 + d * 2]
            second = lengths_ref[m * 4 + d * 2 + 1]
            for j in range(2):
                modality, block = route_of(routes_ref, d, m, j)
                rows = slice((m * 2 + j) * ROWS, (m * 2 + j + 1) * ROWS)
                limit = jnp.where(modality == 0, first + second - j * ROWS, (first, second)[j])
                at_block = aligned(block * ROWS, ROWS)
                picked = jnp.where(
                    modality == d,
                    cot_mine[0, m, at_block, :].astype(F32),
                    cot_other[m, at_block, :].astype(F32),
                )
                picked = jnp.where(iota(picked.shape, 0) < limit, picked, 0.0).astype(BF16)
                cot_ref[rows, :] = picked
                ge_ref[rows, :] = dot_nt(picked, post_ref[modality]).astype(BF16)
        enc_ref[...] = mid_ref[...] + vec_ref[BFO : BFO + 1, :]
        gh_ref[...] = jnp.zeros_like(gh_ref)

    bias_row = vec_ref[pl.ds(BFI + half_ref[0] * 2 + step, 1), :]
    ffn_chunk(h2_ref, ge_ref, win_ref, wout_ref, bias_row, act, gb, h2t, dwout_ref, dwin_ref, dbin_ref)
    for n in range(D // 256):
        cols = slice(n * 256, (n + 1) * 256)
        enc_ref[:, cols] += dot(act[...], wout_ref[:, cols])
        gh_ref[:, cols] += dot_nt(gb[...], win_ref[cols, :])


def ffn_second_kernel(
    half_ref,
    h2_ref, vec_ref, ge_ref, enc_in, gh_in, win_ref, wout_ref,
    enc_ref, gh_ref, dwout_ref, dwin_ref, dbin_ref,
    act, gb, h2t, total,
):
    step = pl.program_id(0)

    @pl.when(step == 0)
    def _():
        h2t[...] = jnp.transpose(h2_ref[...])
        total[...] = enc_in[...]
        gh_ref[...] = gh_in[...]

    bias_row = vec_ref[pl.ds(BFI + half_ref[0] * 2 + step, 1), :]
    ffn_chunk(h2_ref, ge_ref, win_ref, wout_ref, bias_row, act, gb, h2t, dwout_ref, dwin_ref, dbin_ref)
    for n in range(D // 256):
        cols = slice(n * 256, (n + 1) * 256)
        total[:, cols] += dot(act[...], wout_ref[:, cols])
        gh_ref[:, cols] += dot_nt(gb[...], win_ref[cols, :])

    @pl.when(step == pl.num_programs(0) - 1)
    def _():
        enc_ref[...] = total[...].astype(BF16)


def whole_block(shape):
    return pl.BlockSpec(shape, lambda *_: (0,) * len(shape))


def ffn_specs():
    weights = [
        pl.BlockSpec((D, CHUNK), lambda i, half, *_: (0, half[0] * 2 + i)),
        pl.BlockSpec((CHUNK, D), lambda i, half, *_: (half[0] * 2 + i, 0)),
    ]
    grads = [
        pl.BlockSpec((CHUNK, D), lambda i, *_: (i, 0)),
        pl.BlockSpec((D, CHUNK), lambda i, *_: (0, i)),
        pl.BlockSpec((1, 1, CHUNK), lambda i, *_: (i, 0, 0)),
    ]
    grad_shapes = [
        jax.ShapeDtypeStruct((2 * CHUNK, D), BF16),
        jax.ShapeDtypeStruct((D, 2 * CHUNK), BF16),
        jax.ShapeDtypeStruct((2, 1, CHUNK), F32),
    ]
    return weights, grads, grad_shapes


FFN_COST = pl.CostEstimate(flops=7_500_000_000, bytes_accessed=24_000_000, transcendentals=1_600_000)


def ffn_first(half, d, routes, lengths, h2, mid, vecs, cot_mine, cot_other, post, w_in, w_out):
    rows = MICRO * SEQ
    weights, grads, grad_shapes = ffn_specs()
    return pl.pallas_call(
        ffn_first_kernel,
        out_shape=[
            jax.ShapeDtypeStruct((rows, D), F32),
            jax.ShapeDtypeStruct((rows, D), F32),
            jax.ShapeDtypeStruct((rows, D), BF16),
            jax.ShapeDtypeStruct((rows, OUT), BF16),
        ] + grad_shapes,
        grid_spec=pltpu.PrefetchScalarGridSpec(
            num_scalar_prefetch=4,
            grid=(2,),
            in_specs=[
                whole_block((rows, D)), whole_block((rows, D)), whole_block(vecs.shape),
                whole_block(cot_mine.shape), whole_block(cot_other.shape), whole_block(post.shape),
            ] + weights,
            out_specs=[
                whole_block((rows, D)), whole_block((rows, D)), whole_block((rows, D)), whole_block((rows, OUT)),
            ] + grads,
            scratch_shapes=[
                pltpu.VMEM((rows, CHUNK), BF16), pltpu.VMEM((rows, CHUNK), BF16), pltpu.VMEM((D, rows), BF16),
            ],
        ),
        compiler_params=params(("arbitrary",)),
        cost_estimate=FFN_COST,
        name="ffn_first",
    )(half, d, routes, lengths, h2, mid, vecs, cot_mine, cot_other, post, w_in, w_out)


def ffn_second(half, h2, vecs, ge, enc, gh, w_in, w_out):
    rows = MICRO * SEQ
    weights, grads, grad_shapes = ffn_specs()
    return pl.pallas_call(
        ffn_second_kernel,
        out_shape=[
            jax.ShapeDtypeStruct((rows, D), BF16),
            jax.ShapeDtypeStruct((rows, D), F32),
        ] + grad_shapes,
        grid_spec=pltpu.PrefetchScalarGridSpec(
            num_scalar_prefetch=1,
            grid=(2,),
            in_specs=[
                whole_block((rows, D)), whole_block(vecs.shape), whole_block((rows, D)),
                whole_block((rows, D)), whole_block((rows, D)),
            ] + weights,
            out_specs=[whole_block((rows, D)), whole_block((rows, D))] + grads,
            scratch_shapes=[
                pltpu.VMEM((rows, CHUNK), BF16), pltpu.VMEM((rows, CHUNK), BF16), pltpu.VMEM((D, rows), BF16),
                pltpu.VMEM((rows, D), F32),
            ],
        ),
        compiler_params=params(("arbitrary",)),
        cost_estimate=FFN_COST,
        name="ffn_second",
    )(half, h2, vecs, ge, enc, gh, w_in, w_out)


def column_sum(values):
    return jnp.sum(values, axis=0, keepdims=True)


def attend_back_kernel(
    gh_ref, mid_ref, ge_ref, vec_ref, wao_ref, qkv_ref, pt_ref, bucket_ref,
    gm_ref, gbr_ref, gqkv_ref, rel_ref, sums_ref,
    gctx, frow,
):
    sums_ref[...] = jnp.zeros_like(sums_ref)
    frow[...] = jnp.zeros_like(frow)

    def second_norm(r, _):
        rows = aligned(r * ROWS, ROWS)
        normed, inverse = normalise(mid_ref[rows, :])
        grad = gh_ref[rows, :]
        ge = ge_ref[rows, :].astype(F32)
        gm = ge + norm_back(grad, normed, inverse, vec_ref[G2 : G2 + 1, :])
        gm_ref[rows, :] = gm
        low = gm.astype(BF16)
        gbr_ref[rows, :] = low
        sums_ref[0:1, :] += column_sum(grad * normed)
        sums_ref[1:2, :] += column_sum(grad)
        sums_ref[2:3, :] += column_sum(low.astype(F32))
        sums_ref[3:4, :] += column_sum(ge)
        return 0

    lax.fori_loop(0, MICRO * SEQ // ROWS, second_norm, 0)
    for n in range(3):
        cols = slice(n * 256, (n + 1) * 256)
        gctx[:, cols] = dot_nt(gbr_ref[...], wao_ref[cols, :]).astype(BF16)
    low, high = head_masks()

    def attention(pair, _):
        at_q = aligned(pair * 128, 128)
        at_k = aligned(D + pair * 128, 128)
        at_v = aligned(2 * D + pair * 128, 128)
        grads = [[jnp.zeros((SEQ, 128), F32)] * 3 for _ in range(MICRO)]
        for s, keep in enumerate((low, high)):
            both = None
            for m in range(MICRO):
                rows = slice(m * SEQ, (m + 1) * SEQ)
                q = qkv_ref[rows, at_q]
                k = qkv_ref[rows, at_k]
                v = qkv_ref[rows, at_v]
                gc = gctx[rows, at_q]
                weights = pt_ref[m * HEADS + 2 * pair + s]
                wide = weights.astype(F32)
                gp = dot_nt(v * keep, gc)
                inner = jnp.sum(gp * wide, axis=0, keepdims=True)
                gs = wide * (gp - inner)
                both = gs if both is None else both + gs
                scaled = (gs * HEAD_DIM ** (-0.5)).astype(BF16)
                gq, gk, gv = grads[m]
                grads[m] = [
                    gq + dot_tn(scaled, k * keep),
                    gk + dot(scaled, q * keep),
                    gv + dot(weights, gc * keep),
                ]
            acc = None
            for a in range(SEQ // 8):
                part = jnp.concatenate([both[8 * a : 8 * a + 8, :], jnp.zeros((8, SEQ), F32)], axis=1)
                part = pltpu.roll(part, 2 * SEQ - 8 * a, 1) if a else part
                acc = part if acc is None else acc + part
            for bit in (1, 2, 4):
                moved = pltpu.roll(acc, 2 * SEQ - bit, 1)
                acc = jnp.where((iota(acc.shape, 0) & bit) != 0, moved, acc)
            frow[pl.ds(2 * pair + s, 1), :] = jnp.sum(acc, axis=0, keepdims=True)
        for m in range(MICRO):
            rows = slice(m * SEQ, (m + 1) * SEQ)
            for at, grad in zip((at_q, at_k, at_v), grads[m]):
                gqkv_ref[rows, at] = grad.astype(BF16)
        return 0

    lax.fori_loop(0, HEADS // 2, attention, 0)
    hot = (iota((160, 2 * SEQ), 0) == bucket_ref[...]).astype(F32).astype(BF16)
    rest = frow[...]
    rel = jnp.zeros((16, 160), F32)
    for _ in range(3):
        term = rest.astype(BF16)
        rest = rest - term.astype(F32)
        rel = rel + dot_nt(term, hot)
    rel_ref[...] = rel
    sums_ref[4:5, :] = column_sum(gqkv_ref[:, 0:D].astype(F32))
    sums_ref[5:6, :] = column_sum(gqkv_ref[:, 2 * D : 3 * D].astype(F32))


def attend_back(gh, mid, ge, vecs, w_ao, qkv, pt, bucket_row):
    rows = MICRO * SEQ
    return pl.pallas_call(
        attend_back_kernel,
        out_shape=[
            jax.ShapeDtypeStruct((rows, D), F32),
            jax.ShapeDtypeStruct((rows, D), BF16),
            jax.ShapeDtypeStruct((rows, 3 * D), BF16),
            jax.ShapeDtypeStruct((16, 160), F32),
            jax.ShapeDtypeStruct((8, D), F32),
        ],
        in_specs=[vmem()] * 8,
        out_specs=[vmem()] * 5,
        scratch_shapes=[pltpu.VMEM((rows, D), BF16), pltpu.VMEM((16, 2 * SEQ), F32)],
        compiler_params=params(),
        cost_estimate=pl.CostEstimate(flops=5_000_000_000, bytes_accessed=16_000_000, transcendentals=0),
        name="attend_back",
    )(gh, mid, ge, vecs, w_ao, qkv, pt, bucket_row)


def tail_kernel(
    d_ref, routes_ref,
    gqkv_ref, h1_ref, x_ref, gm_ref, vec_ref, gbr_ref, ctx_ref, enc_ref, cot_ref, feats_ref, ids_ref,
    rel_ref, sums_ref, dbin_other, dbin_mine, wqkv_ref,
    other_ref, mine_ref, eg_ref, small_ref,
    left, rest,
):
    d = d_ref[0]
    outs = (other_ref, mine_ref)
    halves = (1 - d, d)
    small_ref[...] = jnp.zeros_like(small_ref)
    left[...] = jnp.transpose(h1_ref[...])
    for out, half in zip(outs, halves):
        for n in range(3):
            cols = aligned(half * 1152 + n * 384, 128)
            cols = pl.ds(pl.multiple_of(half * 1152 + n * 384, 128), 384)
            out[:, n * 384 : (n + 1) * 384] = dot(left[...], gqkv_ref[:, cols]).astype(BF16)
    left[...] = jnp.transpose(ctx_ref[...])
    for out, half in zip(outs, halves):
        cols = pl.ds(pl.multiple_of(half * 384, 128), 384)
        out[:, 1152:1536] = dot(left[...], gbr_ref[:, cols]).astype(BF16)

    def first_norm(r, _):
        rows = aligned(r * ROWS, ROWS)
        normed, inverse = normalise(x_ref[rows, :].astype(F32))
        grad = dot_nt(gqkv_ref[rows, :], wqkv_ref[...])
        eg = gm_ref[rows, :] + norm_back(grad, normed, inverse, vec_ref[G1 : G1 + 1, :])
        eg_ref[rows, :] = eg.astype(BF16)
        small_ref[G1 : G1 + 1, :] += column_sum(grad * normed)
        small_ref[S1 : S1 + 1, :] += column_sum(grad)
        return 0

    lax.fori_loop(0, MICRO * SEQ // ROWS, first_norm, 0)
    for out in outs:
        out[0:512, 1536:1920] = jnp.zeros((512, 384), BF16)
    rest[...] = jnp.zeros_like(rest)
    for m in range(MICRO):
        modality, _ = route_of(routes_ref, d, m, 0)
        rows = slice(m * SEQ, (m + 1) * SEQ)
        blocks = [route_of(routes_ref, d, m, j)[1] for j in range(2)]
        post = dot_tn(cot_ref[rows, :], enc_ref[rows, :])

        @pl.when(modality == 0)
        def _(m=m, rows=rows, blocks=blocks, post=post):
            raw = jnp.concatenate(
                [feats_ref[m, aligned(block * ROWS, ROWS), :] for block in blocks], axis=0
            )
            raw = jnp.transpose(raw)
            for out, half in zip(outs, halves):
                cols = pl.ds(pl.multiple_of(half * 384, 128), 384)
                grown = out[0:512, 1536:1920].astype(F32) + dot(raw, eg_ref[rows, cols])
                out[0:512, 1536:1920] = grown.astype(BF16)
            small_ref[SB : SB + 1, :] += column_sum(eg_ref[rows, :].astype(F32))
            rest[OUT : 2 * OUT, :] += post

        @pl.when(modality != 0)
        def _(m=m, rows=rows, blocks=blocks, post=post):
            table = jnp.zeros((ROWS, D), F32)
            for j, block in enumerate(blocks):
                hot = onehot_vocab(ids_ref, m, block)
                table = table + dot(hot, eg_ref[m * SEQ + j * ROWS : m * SEQ + (j + 1) * ROWS, :])
            rest[0:OUT, :] += table[0:OUT, :]
            rest[2 * OUT : 3 * OUT, :] += post

    for out, half in zip(outs, halves):
        cols = pl.ds(pl.multiple_of(half * 384, 128), 384)
        out[512:768, 1536:1920] = rest[:, cols].astype(BF16)
    for at, row in ((G2, 0), (S2, 1), (BAO, 2), (BFO, 3), (BQ, 4), (BV, 5)):
        small_ref[at : at + 1, :] = sums_ref[row : row + 1, :]
    for dbin, half in ((dbin_other, halves[0]), (dbin_mine, halves[1])):
        for i in range(2):
            small_ref[pl.ds(BFI + half * 2 + i, 1), :] = dbin[i]
    small_ref[REL_ROW : REL_ROW + 16, 0:160] = rel_ref[...]


def tail(d, routes, gqkv, h1, x, gm, vecs, gbr, ctx, enc, cot, feats, ids, rel, sums, dbin_other, dbin_mine, w_qkv):
    rows = MICRO * SEQ
    return pl.pallas_call(
        tail_kernel,
        out_shape=[
            jax.ShapeDtypeStruct((D, 1920), BF16),
            jax.ShapeDtypeStruct((D, 1920), BF16),
            jax.ShapeDtypeStruct((rows, D), BF16),
            jax.ShapeDtypeStruct((SMALL_ROWS, D), F32),
        ],
        in_specs=[smem()] * 2 + [vmem()] * 16,
        out_specs=[vmem()] * 4,
        scratch_shapes=[pltpu.VMEM((D, rows), BF16), pltpu.VMEM((256, D), F32)],
        compiler_params=params(),
        cost_estimate=pl.CostEstimate(flops=6_000_000_000, bytes_accessed=20_000_000, transcendentals=0),
        name="tail",
    )(d, routes, gqkv, h1, x, gm, vecs, gbr, ctx, enc, cot, feats, ids, rel, sums, dbin_other, dbin_mine, w_qkv)


class Links:
    def __init__(self, mesh):
        self.nb = mesh.shape["batch"]
        self.nz = self.nb // 4
        self.c = lax.axis_index("mod")
        batch = lax.axis_index("batch")
        low, high = batch % 2, (batch // 2) % 2
        self.z = batch // 4
        self.b1 = jnp.where(self.c == 0, low, high)
        self.b2 = jnp.where(self.c == 0, high, low)

    def pairs(self, step):
        return [
            (c * self.nb + b, c2 * self.nb + b2)
            for c in range(2)
            for b in range(self.nb)
            for c2, b2 in [step(c, b)]
        ]

    def core(self, v):
        return lax.ppermute(v, AXES, self.pairs(lambda c, b: (1 - c, b)))

    def first(self, v):
        return lax.ppermute(v, AXES, self.pairs(lambda c, b: (c, b ^ (1 if c == 0 else 2))))

    def second(self, v):
        return lax.ppermute(v, AXES, self.pairs(lambda c, b: (c, b ^ (2 if c == 0 else 1))))

    def along(self, v, k):
        return lax.ppermute(v, AXES, self.pairs(lambda c, b: (c, (b + 4 * k) % self.nb)))


def pick(v, i):
    return lax.dynamic_index_in_dim(v, i, 0, keepdims=False)


def add(*terms):
    total = terms[0].astype(F32)
    for term in terms[1:]:
        total = total + term.astype(F32)
    return total.astype(BF16)


def reduce_scatter(links, terms):
    rows, cols = terms[0].shape
    halves = [t.reshape(2, rows // 2, cols) for t in terms]
    got = links.first(add(*[pick(t, 1 - links.b1) for t in halves]))
    quarters = [pick(t, links.b1).reshape(2, rows // 4, cols) for t in halves] + [got.reshape(2, rows // 4, cols)]
    got = links.second(add(*[pick(t, 1 - links.b2) for t in quarters]))
    quarter = add(*[pick(t, links.b2) for t in quarters], got)
    parts = quarter.reshape(links.nz, rows // 4 // links.nz, cols)
    got = [links.along(pick(parts, (links.z + k) % links.nz), k) for k in range(1, links.nz)]
    return add(pick(parts, links.z), *got)


def all_gather(links, part):
    ring = jnp.concatenate([part] + [links.along(part, k) for k in range(1, links.nz)], axis=0)
    across = links.second(ring)
    mine = [ring, across, links.first(ring), links.first(across)]
    return mine + [links.core(v) for v in mine]


def place_kernel(nz, widths, z_ref, table_ref, *refs):
    ins, outs = refs[:8], refs[8:]
    step = pl.program_id(0)
    part = ins[0].shape[0] // nz
    for i, ref in enumerate(ins):

        @pl.when(step == i)
        def _(ref=ref):
            for k in range(nz):
                at = lax.rem(z_ref[0] + nz - k, nz)
                rows = pl.ds(pl.multiple_of(at * part, 8), part)
                start = 0
                for out, width in zip(outs, widths):
                    out[rows, :] = ref[k * part : (k + 1) * part, start : start + width].astype(F32)
                    start += width


def place(links, gathered, widths, by_rows):
    quarter, cols = gathered[0].shape
    b1, b2, c = links.b1, links.b2, links.c
    spots = []
    for core, first, second in ((c, b1, b2), (1 - c, b2, b1)):
        for i, j in ((0, 0), (0, 1), (1, 0), (1, 1)):
            spots += [core, (first ^ i) * 2 + (second ^ j)]
    table = jnp.stack(spots).astype(jnp.int32)
    if by_rows:
        out_map = lambda s, z, t: (t[2 * s] * 4 + t[2 * s + 1], 0)
        shapes = [(8 * quarter, w) for w in widths]
    else:
        out_map = lambda s, z, t: (t[2 * s + 1], t[2 * s])
        shapes = [(4 * quarter, 2 * w) for w in widths]
    return pl.pallas_call(
        functools.partial(place_kernel, links.nz, widths),
        out_shape=[jax.ShapeDtypeStruct(s, F32) for s in shapes],
        grid_spec=pltpu.PrefetchScalarGridSpec(
            num_scalar_prefetch=2,
            grid=(8,),
            in_specs=[whole_block((quarter, cols))] * 8,
            out_specs=[pl.BlockSpec((quarter, w), out_map) for w in widths],
        ),
        compiler_params=params(("arbitrary",)),
        cost_estimate=pl.CostEstimate(flops=1_000_000, bytes_accessed=48 * quarter * cols, transcendentals=0),
        name="place",
    )(links.z.reshape(1).astype(jnp.int32), table, *gathered)


def sum_small(links, small):
    total = small + links.core(small)
    total = total + links.first(total)
    total = total + links.second(total)
    moved = [links.along(total, k) for k in range(1, links.nz)]
    for m in moved:
        total = total + m
    return total


def padded(v, rows):
    short = -v.shape[0] % rows
    return jnp.pad(v, ((0, short), (0, 0))) if short else v


def on_device(
    mesh,
    speech_feats, text_ids, routes, lengths, buckets, post_cot,
    ln1_gain, ln1_bias, w_qkv, bias_qv, rel_table, w_attn_out, bias_attn_out,
    ln2_gain, ln2_bias, w_ffn_in, bias_ffn_in, w_ffn_out, bias_ffn_out,
    speech_proj, speech_bias, text_table, post_weight,
):
    links = Links(mesh)
    d = links.c.reshape(1).astype(jnp.int32)
    cot_other = links.core(post_cot[0])
    routes = routes.reshape(-1)
    lengths = lengths.reshape(-1)
    vecs = jnp.concatenate([
        ln1_gain, ln1_bias, bias_qv.reshape(-1), bias_attn_out, ln2_gain, ln2_bias, bias_ffn_out, speech_bias,
        bias_ffn_in, jnp.zeros((3 * D,), BF16),
    ]).astype(F32).reshape(16, D)
    bucket_row = jnp.concatenate([buckets[SEQ - 1 :], buckets[:1], buckets[: SEQ - 1]]).reshape(1, 2 * SEQ)
    rel = jnp.pad(jnp.transpose(rel_table), ((0, 4), (0, 96)))
    x, h1, qkv, pt, ctx, mid, h2 = front(
        d, routes, lengths, speech_feats, text_ids, bucket_row, rel, speech_proj, text_table, vecs, w_qkv, w_attn_out
    )
    enc, gh, ge, cot, dwout_other, dwin_other, dbin_other = ffn_first(
        1 - d, d, routes, lengths, h2, mid, vecs, post_cot, cot_other, post_weight, w_ffn_in, w_ffn_out
    )
    out_got = links.core(dwout_other)
    in_got = links.core(dwin_other)
    enc, gh, dwout, dwin, dbin = ffn_second(d, h2, vecs, ge, enc, gh, w_ffn_in, w_ffn_out)
    align = 4 * links.nz * 8
    out_part = reduce_scatter(links, [padded(dwout, align), padded(out_got, align)])
    in_part = reduce_scatter(links, [padded(dwin, align), padded(in_got, align)])
    gm, gbr, gqkv, drel, sums = attend_back(gh, mid, ge, vecs, w_attn_out, qkv, pt, bucket_row)
    other, mine, eg, small = tail(
        d, routes, gqkv, h1, x, gm, vecs, gbr, ctx, enc, cot, speech_feats, text_ids, drel, sums,
        dbin_other, dbin, w_qkv,
    )
    rest_got = links.core(other)
    small = sum_small(links, small)
    rest_part = reduce_scatter(links, [padded(mine, align), padded(rest_got, align)])
    (g_out,) = place(links, all_gather(links, out_part), (D,), True)
    (g_in,) = place(links, all_gather(links, in_part), (FF // 2,), False)
    g_qkv, g_ao, g_rest = place(links, all_gather(links, rest_part), (1152, 384, 384), False)
    g_post = g_rest[512 + OUT : 512 + 3 * OUT].reshape(2, OUT, D).transpose(0, 2, 1)
    rows = text_ids.shape[0]
    return (
        enc.reshape(rows, SEQ, D),
        eg.reshape(rows, SEQ, D),
        small[G1],
        small[S1],
        g_qkv[:D],
        small[BQ : BQ + 2],
        small[REL_ROW : REL_ROW + HEADS, 0 : rel_table.shape[0]].T,
        g_ao[:D],
        small[BAO],
        small[G2],
        small[S2],
        g_in[:D],
        small[BFI : BFI + 4].reshape(FF),
        g_out[:FF],
        small[BFO],
        g_rest[:512],
        small[SB],
        g_rest[512 : 512 + OUT],
        g_post,
    )


def solution(mesh):
    batch = P(None, "batch", None)
    rows = P(None, AXES, None)
    return jax.shard_map(
        functools.partial(on_device, mesh),
        mesh=mesh,
        in_specs=(
            batch, P(None, "batch"), P(None, "batch", None, None), P(None, "batch", None, None), P(),
            P("mod", None, "batch", None),
        ) + (P(),) * 17,
        out_specs=(rows, rows) + (P(),) * 17,
        check_vma=False,
    )
```

profile of v0, /device:TPU:0, one launch (start us, length us, event | category | flops | bytes accessed | tf_op | source)
XLA Modules:
  0.0 343.4 jit_solution(575791210741185)
XLA Ops:
  18.8 20.8 %front.1 = (bf16[512,768]{1,0:T(8,128)(2,1)}, bf16[512,768]{1,0:T(8,128)(2,1)}, bf16[512,2304]{1,0:T(8,128)(2,1)}, bf16[24,256,256]{2,1,0:T(8,128)(2,1)}, bf16[5...) custom-call(s32[1]{0:T(128)} %bitcast.d_ref.half_ref, s32[8]{0:T(128)} %reshape.186.routes_ref, ...), custom_call_target="tpu_custom_call" | custom-call | flops 4000000000 | bytes 20000000 | tf_op jit(solution)/shard_map/front/pallas_call | solution.py:212
  41.3 14.5 %ffn_first.1 = (f32[512,768]{1,0:T(8,128)}, f32[512,768]{1,0:T(8,128)}, bf16[512,768]{1,0:T(8,128)(2,1)}, bf16[512,81]{1,0:T(8,128)(2,1)}, bf16[1536,768]{1,0:T(...) custom-call(s32[1]{0:T(128)S(6)} %sub.15.half_ref, s32[1]{0:T(128)} %bitcast.d_ref.half_ref, ...), custom_call_target="tpu_custom_call" | custom-call | flops 7500000256 | bytes 24000000 | tf_op jit(solution)/shard_map/ffn_first/pallas_call | solution.py:350
  55.9 14.1 %ffn_second.1 = (bf16[512,768]{1,0:T(8,128)(2,1)}, f32[512,768]{1,0:T(8,128)}, bf16[1536,768]{1,0:T(8,128)(2,1)}, bf16[768,1536]{1,0:T(8,128)(2,1)}, f32[2,1,768]{2,1,0:T(1,128)}) custom-call(s32[1]{0:T(128)} %bitcast.d_ref.half_ref, bf16[512,768]{1,0:T(8,128)(2,1)} %get-tuple-element.50.h2_ref, f32[16,768]{1,0:T(8,128)} %reshape.213.vec_ref, ...), custom_call_target="tpu_custom_call" | custom-call | flops 7500000256 | bytes 24000000 | tf_op jit(solution)/shard_map/ffn_second/pallas_call | solution.py:381
  70.0 17.3 %attend_back.1 = (f32[512,768]{1,0:T(8,128)}, bf16[512,768]{1,0:T(8,128)(2,1)}, bf16[512,2304]{1,0:T(8,128)(2,1)}, f32[16,160]{1,0:T(8,128)}, f32[8,768]{1,0:T(8,128)}) custom-call(f32[512,768]{1,0:T(8,128)} %get-tuple-element.56.gh_ref, f32[512,768]{1,0:T(8,128)} %get-tuple-element.51.mid_ref, bf16[512,768]{1,0:T(8,128)(2,1)} %get-tuple-element.52.ge_ref, ...), custom_call_target="tpu_custom_call" | custom-call | flops 5000000000 | bytes 16000000 | tf_op jit(solution)/shard_map/attend_back/pallas_call | solution.py:495
  87.4 18.2 %tail.1 = (bf16[768,1920]{1,0:T(8,128)(2,1)}, bf16[768,1920]{1,0:T(8,128)(2,1)}, bf16[512,768]{1,0:T(8,128)(2,1)}, f32[32,768]{1,0:T(8,128)}) custom-call(s32[1]{0:T(128)} %bitcast.d_ref.half_ref, s32[8]{0:T(128)} %reshape.186.routes_ref, bf16[512,2304]{1,0:T(8,128)(2,1)} %get-tuple-element.59.gqkv_ref, bf16[512,768]{1,0:T(8,128)(2,1)} %get-tuple-element.60.h1_ref, ...), custom_call_target="tpu_custom_call" | custom-call | flops 6000000000 | bytes 20000000 | tf_op jit(solution)/shard_map/tail/pallas_call | solution.py:590
  106.6 2.0 fusion.2
  108.6 2.9 collective-permute-start.24
  111.5 1.3 constant_dynamic-slice_fusion.3
  112.9 1.9 collective-permute-done.1
  114.8 3.2 collective-permute-start.2
  118.1 8.7 %collective-permute-done.2 = f32[32,768]{1,0:T(8,128)S(1)} collective-permute-done((f32[32,768]{1,0:T(8,128)S(1)}, f32[32,768]{1,0:T(8,128)S(1)}, u32[]{:S(2)}, u32[]{:S(2)}) %collective-permute-start.2) | collective-permute-done | bytes 98336 | tf_op jit(solution)/shard_map/ppermute | solution.py:630
  126.8 1.8 collective-permute-start.3
  128.6 1.6 fusion.3
  130.3 1.5 collective-permute-start.40
  134.8 4.2 %collective-permute-start.6 = (f32[32,768]{1,0:T(8,128)S(1)}, f32[32,768]{1,0:T(8,128)S(1)}, u32[]{:S(2)}, u32[]{:S(2)}) collective-permute-start(f32[32,768]{1,0:T(8,128)S(1)} %add.272), channel_id=1, source_target_pairs={{0,12},{1,13},{2,14},{3,15},{4,0},{5,1},{6,2},{7,3},{8,4},{9,5},{1... | collective-permute-start | bytes 294920 | tf_op jit(solution)/shard_map/ppermute | solution.py:636
  139.1 1.3 constant_dynamic-slice_fusion.2
  140.5 12.3 %collective-permute-done.40 = bf16[768,768]{1,0:T(8,128)(2,1)S(1)} collective-permute-done((bf16[768,768]{1,0:T(8,128)(2,1)S(1)}, bf16[768,768]{1,0:T(8,128)(2,1)S(1)}, u32[]{:S(2)}, u32[]{:S(2)}) %collective-permute-start.40) | collective-permute-done | bytes 1179680 | tf_op jit(solution)/shard_map/ppermute | solution.py:630
  153.8 4.3 %collective-permute-start.28 = (bf16[48,1536]{1,0:T(8,128)(2,1)S(1)}, bf16[48,1536]{1,0:T(8,128)(2,1)S(1)}, u32[]{:S(2)}, u32[]{:S(2)}) collective-permute-start(bf16[48,1536]{1,0:T(8,128)(2,1)S(1)} %get-tuple-element.114), channel_id=1, source_target_pairs={{0,12},{1,13},{2,14},{3,15},{4,0},{5,1},{6,2},{7,3},{8,4},{9,5},{1... | collective-permute-start | bytes 442376 | tf_op jit(solution)/shard_map/ppermute | solution.py:636
  158.0 16.9 %collective-permute-done.8 = bf16[384,1920]{1,0:T(8,128)(2,1)S(1)} collective-permute-done((bf16[384,1920]{1,0:T(8,128)(2,1)S(1)}, bf16[384,1920]{1,0:T(8,128)(2,1)S(1)}, u32[]{:S(2)}, u32[]{:S(2)}) %collective-permute-start.8) | collective-permute-done | bytes 1474592 | tf_op jit(solution)/shard_map/ppermute | solution.py:630
  175.0 1.5 collective-permute-start.26
  177.8 4.3 %collective-permute-done.26 = bf16[48,1536]{1,0:T(8,128)(2,1)S(1)} collective-permute-done((bf16[48,1536]{1,0:T(8,128)(2,1)S(1)}, bf16[48,1536]{1,0:T(8,128)(2,1)S(1)}, u32[]{:S(2)}, u32[]{:S(2)}) %collective-permute-start.26) | collective-permute-done | bytes 147488 | tf_op jit(solution)/shard_map/ppermute | solution.py:636
  182.2 2.0 collective-permute-start.31
  185.6 4.1 %collective-permute-done.31 = bf16[48,1536]{1,0:T(8,128)(2,1)S(1)} collective-permute-done((bf16[48,1536]{1,0:T(8,128)(2,1)S(1)}, bf16[48,1536]{1,0:T(8,128)(2,1)S(1)}, u32[]{:S(2)}, u32[]{:S(2)}) %collective-permute-start.31) | collective-permute-done | bytes 147488 | tf_op jit(solution)/shard_map/ppermute | solution.py:636
  189.7 4.8 %collective-permute-start.5 = (f32[32,768]{1,0:T(8,128)S(1)}, f32[32,768]{1,0:T(8,128)S(1)}, u32[]{:S(2)}, u32[]{:S(2)}) collective-permute-start(f32[32,768]{1,0:T(8,128)S(1)} %add.272), channel_id=1, source_target_pairs={{0,8},{1,9},{2,10},{3,11},{4,12},{5,13},{6,14},{7,15},{8,0},{9,1},... | collective-permute-start | bytes 294920 | tf_op jit(solution)/shard_map/ppermute | solution.py:636
  194.5 3.6 %collective-permute-done.30 = bf16[48,1536]{1,0:T(8,128)(2,1)S(1)} collective-permute-done((bf16[48,1536]{1,0:T(8,128)(2,1)S(1)}, bf16[48,1536]{1,0:T(8,128)(2,1)S(1)}, u32[]{:S(2)}, u32[]{:S(2)}) %collective-permute-start.30) | collective-permute-done | bytes 147488 | tf_op jit(solution)/shard_map/ppermute | solution.py:636
  198.1 5.3 %collective-permute-start.43 = (bf16[96,768]{1,0:T(8,128)(2,1)S(1)}, bf16[96,768]{1,0:T(8,128)(2,1)S(1)}, u32[]{:S(2)}, u32[]{:S(2)}) collective-permute-start(bf16[96,768]{1,0:T(8,128)(2,1)S(1)} %get-tuple-element.112), channel_id=1, source_target_pairs={{0,8},{1,9},{2,10},{3,11},{4,12},{5,13},{6,14},{7,15},{8,0},{9,1},... | collective-permute-start | bytes 442376 | tf_op jit(solution)/shard_map/ppermute | solution.py:636
  204.6 1.5 collective-permute-done.44
  206.1 3.8 %collective-permute-start.12 = (bf16[48,1920]{1,0:T(8,128)(2,1)S(1)}, bf16[48,1920]{1,0:T(8,128)(2,1)S(1)}, u32[]{:S(2)}, u32[]{:S(2)}) collective-permute-start(bf16[48,1920]{1,0:T(8,128)(2,1)S(1)} %get-tuple-element.108), channel_id=1, source_target_pairs={{0,12},{1,13},{2,14},{3,15},{4,0},{5,1},{6,2},{7,3},{8,4},{9,5},{1... | collective-permute-start | bytes 552968 | tf_op jit(solution)/shard_map/ppermute | solution.py:636
  209.9 8.1 %collective-permute-done.43 = bf16[96,768]{1,0:T(8,128)(2,1)S(1)} collective-permute-done((bf16[96,768]{1,0:T(8,128)(2,1)S(1)}, bf16[96,768]{1,0:T(8,128)(2,1)S(1)}, u32[]{:S(2)}, u32[]{:S(2)}) %collective-permute-start.43) | collective-permute-done | bytes 147488 | tf_op jit(solution)/shard_map/ppermute | solution.py:636
  218.1 3.9 %collective-permute-start.47 = (bf16[96,768]{1,0:T(8,128)(2,1)S(1)}, bf16[96,768]{1,0:T(8,128)(2,1)S(1)}, u32[]{:S(2)}, u32[]{:S(2)}) collective-permute-start(bf16[96,768]{1,0:T(8,128)(2,1)S(1)} %fusion.14), channel_id=1, source_target_pairs={{0,12},{1,13},{2,14},{3,15},{4,0},{5,1},{6,2},{7,3},{8,4},{9,5},{1... | collective-permute-start | bytes 442376 | tf_op jit(solution)/shard_map/ppermute | solution.py:636
  222.7 6.8 %collective-permute-start.46 = (bf16[96,768]{1,0:T(8,128)(2,1)S(1)}, bf16[96,768]{1,0:T(8,128)(2,1)S(1)}, u32[]{:S(2)}, u32[]{:S(2)}) collective-permute-start(bf16[96,768]{1,0:T(8,128)(2,1)S(1)} %fusion.14), channel_id=1, source_target_pairs={{0,8},{1,9},{2,10},{3,11},{4,12},{5,13},{6,14},{7,15},{8,0},{9,1},... | collective-permute-start | bytes 442376 | tf_op jit(solution)/shard_map/ppermute | solution.py:636
  229.4 4.4 %collective-permute-done.11 = bf16[48,1920]{1,0:T(8,128)(2,1)S(1)} collective-permute-done((bf16[48,1920]{1,0:T(8,128)(2,1)S(1)}, bf16[48,1920]{1,0:T(8,128)(2,1)S(1)}, u32[]{:S(2)}, u32[]{:S(2)}) %collective-permute-start.11) | collective-permute-done | bytes 184352 | tf_op jit(solution)/shard_map/ppermute | solution.py:636
  235.1 3.9 %collective-permute-start.15 = (bf16[48,1920]{1,0:T(8,128)(2,1)S(1)}, bf16[48,1920]{1,0:T(8,128)(2,1)S(1)}, u32[]{:S(2)}, u32[]{:S(2)}) collective-permute-start(bf16[48,1920]{1,0:T(8,128)(2,1)S(1)} %fusion.11), channel_id=1, source_target_pairs={{0,12},{1,13},{2,14},{3,15},{4,0},{5,1},{6,2},{7,3},{8,4},{9,5},{1... | collective-permute-start | bytes 552968 | tf_op jit(solution)/shard_map/ppermute | solution.py:636
  239.0 7.8 %collective-permute-done.46 = bf16[96,768]{1,0:T(8,128)(2,1)S(1)} collective-permute-done((bf16[96,768]{1,0:T(8,128)(2,1)S(1)}, bf16[96,768]{1,0:T(8,128)(2,1)S(1)}, u32[]{:S(2)}, u32[]{:S(2)}) %collective-permute-start.46) | collective-permute-done | bytes 147488 | tf_op jit(solution)/shard_map/ppermute | solution.py:636
  246.8 2.6 collective-permute-start.13
  249.5 3.1 collective-permute-start.48
  252.6 6.0 %collective-permute-done.14 = bf16[48,1920]{1,0:T(8,128)(2,1)S(1)} collective-permute-done((bf16[48,1920]{1,0:T(8,128)(2,1)S(1)}, bf16[48,1920]{1,0:T(8,128)(2,1)S(1)}, u32[]{:S(2)}, u32[]{:S(2)}) %collective-permute-start.14) | collective-permute-done | bytes 184352 | tf_op jit(solution)/shard_map/ppermute | solution.py:636
  262.2 11.9 %collective-permute-done.49.refs_2_ = bf16[384,768]{1,0:T(8,128)(2,1)S(1)} collective-permute-done((bf16[384,768]{1,0:T(8,128)(2,1)S(1)}, bf16[384,768]{1,0:T(8,128)(2,1)S(1)}, u32[]{:S(2)}, u32[]{:S(2)}) %collective-permute-start.49) | collective-permute-done | bytes 589856 | tf_op jit(solution)/shard_map/ppermute | solution.py:630
  275.3 7.4 %collective-permute-done.34.refs_3_ = bf16[192,1536]{1,0:T(8,128)(2,1)S(1)} collective-permute-done((bf16[192,1536]{1,0:T(8,128)(2,1)S(1)}, bf16[192,1536]{1,0:T(8,128)(2,1)S(1)}, u32[]{:S(2)}, u32[]{:S(2)}) %collective-permute-start.34) | collective-permute-done | bytes 589856 | tf_op jit(solution)/shard_map/ppermute | solution.py:630
  285.3 3.9 %collective-permute-done.50.refs_3_ = bf16[384,768]{1,0:T(8,128)(2,1)} collective-permute-done((bf16[384,768]{1,0:T(8,128)(2,1)S(1)}, bf16[384,768]{1,0:T(8,128)(2,1)}, u32[]{:S(2)}, u32[]{:S(2)}) %collective-permute-start.50) | collective-permute-done | bytes 589856 | tf_op jit(solution)/shard_map/ppermute | solution.py:630
  289.8 7.2 %collective-permute-done.17.refs_2_ = bf16[192,1920]{1,0:T(8,128)(2,1)S(1)} collective-permute-done((bf16[192,1920]{1,0:T(8,128)(2,1)S(1)}, bf16[192,1920]{1,0:T(8,128)(2,1)S(1)}, u32[]{:S(2)}, u32[]{:S(2)}) %collective-permute-start.17) | collective-permute-done | bytes 737312 | tf_op jit(solution)/shard_map/ppermute | solution.py:630
  297.0 7.9 %collective-permute-done.18.refs_3_ = bf16[192,1920]{1,0:T(8,128)(2,1)S(1)} collective-permute-done((bf16[192,1920]{1,0:T(8,128)(2,1)S(1)}, bf16[192,1920]{1,0:T(8,128)(2,1)S(1)}, u32[]{:S(2)}, u32[]{:S(2)}) %collective-permute-start.18) | collective-permute-done | bytes 737312 | tf_op jit(solution)/shard_map/ppermute | solution.py:630
  309.2 1.6 slice_reduce_fusion
  312.2 7.9 %place.4 = f32[768,3072]{1,0:T(8,128)} custom-call(s32[1]{0:T(128)} %bitcast.6.z_ref, s32[16]{0:T(128)} %stack.29.table_ref, bf16[192,1536]{1,0:T(8,128)(2,1)} %copy-done.2, bf16[192,1536]{1,0:T(8,128)(2,1)} %copy-done.8, bf16[192,1536]{1,0:T(8,128)(2,1)} %copy-done.9, bf16[192,1536]{1,0:T(8,128)(2,1)} %copy-done.14, bf16[192,1536]{1,0:T(8,128)(2,1)} %copy-done.10, ...), custom_call_target="tpu_custom_call" | custom-call | flops 1000000 | bytes 14155776 | tf_op jit(solution)/shard_map/place/pallas_call | solution.py:700
  320.1 7.9 %place.5 = f32[3072,768]{1,0:T(8,128)} custom-call(s32[1]{0:T(128)} %bitcast.6.z_ref, s32[16]{0:T(128)} %stack.29.table_ref, bf16[384,768]{1,0:T(8,128)(2,1)} %copy-done.3, bf16[384,768]{1,0:T(8,128)(2,1)} %copy-done.11, bf16[384,768]{1,0:T(8,128)(2,1)} %copy-done.12, bf16[384,768]{1,0:T(8,128)(2,1)} %collective-permute-done.50.refs_3_, ...), custom_call_target="tpu_custom_call" | custom-call | flops 1000000 | bytes 14155776 | tf_op jit(solution)/shard_map/place/pallas_call | solution.py:700
  328.0 8.9 %place.3 = (f32[768,2304]{1,0:T(8,128)}, f32[768,768]{1,0:T(8,128)}, f32[768,768]{1,0:T(8,128)}) custom-call(s32[1]{0:T(128)} %bitcast.6.z_ref, s32[16]{0:T(128)} %stack.29.table_ref, bf16[192,1920]{1,0:T(8,128)(2,1)} %copy-done, bf16[192,1920]{1,0:T(8,128)(2,1)} %copy-done.5, bf16[192,1920]{1,0:T(8,128)(2,1)} %copy-done.6, bf16[192,1920]{1,0:T(8,128)(2,1)} %copy-done.7, ...), custom_call_target="tpu_custom_call" | custom-call | flops 1000000 | bytes 17694720 | tf_op jit(solution)/shard_map/place/pallas_call | solution.py:700
  336.9 2.7 slice.60
  339.5 1.7 slice.62
  (188 shorter events, 46.7 us)
Async XLA Ops:
  1.8 38.8 %collective-permute-start = (bf16[2,512,81]{2,1,0:T(8,128)(2,1)S(1)}, bf16[2,512,81]{2,1,0:T(8,128)(2,1)S(1)}, u32[]{:S(2)}, u32[]{:S(2)}) collective-permute-start(bf16[2,512,81]{2,1,0:T(8,128)(2,1)S(1)} %bitcast.121), channel_id=1, source_target_pairs={{0,16},{1,17},{2,18},{3,19},{4,20},{5,21},{6,22},{7,23},{8,24},{9,... | collective-permute-start | bytes 497672 | tf_op jit(solution)/shard_map/ppermute | solution.py:627
  55.8 50.8 %collective-permute-start.23 = (bf16[768,1536]{1,0:T(8,128)(2,1)}, bf16[768,1536]{1,0:T(8,128)(2,1)}, u32[]{:S(2)}, u32[]{:S(2)}) collective-permute-start(bf16[768,1536]{1,0:T(8,128)(2,1)} %get-tuple-element.77), channel_id=1, source_target_pairs={{0,16},{1,17},{2,18},{3,19},{4,20},{5,21},{6,22},{7,23},{8,24},{9,... | collective-permute-start | bytes 7077896 | tf_op jit(solution)/shard_map/ppermute | solution.py:627
  105.5 27.6 %collective-permute-start.7 = (bf16[768,1920]{1,0:T(8,128)(2,1)}, bf16[768,1920]{1,0:T(8,128)(2,1)S(1)}, u32[]{:S(2)}, u32[]{:S(2)}) collective-permute-start(bf16[768,1920]{1,0:T(8,128)(2,1)} %get-tuple-element.73), channel_id=1, source_target_pairs={{0,16},{1,17},{2,18},{3,19},{4,20},{5,21},{6,22},{7,23},{8,24},{9,... | collective-permute-start | bytes 8847368 | tf_op jit(solution)/shard_map/ppermute | solution.py:627
  106.0 22.6 %collective-permute-start.39 = (bf16[1536,768]{1,0:T(8,128)(2,1)}, bf16[1536,768]{1,0:T(8,128)(2,1)}, u32[]{:S(2)}, u32[]{:S(2)}) collective-permute-start(bf16[1536,768]{1,0:T(8,128)(2,1)} %get-tuple-element.79), channel_id=1, source_target_pairs={{0,16},{1,17},{2,18},{3,19},{4,20},{5,21},{6,22},{7,23},{8,24},{9,... | collective-permute-start | bytes 7077896 | tf_op jit(solution)/shard_map/ppermute | solution.py:627
  108.6 25.5 %collective-permute-start.24 = (bf16[384,1536]{1,0:T(8,128)(2,1)S(1)}, bf16[384,1536]{1,0:T(8,128)(2,1)S(1)}, u32[]{:S(2)}, u32[]{:S(2)}) collective-permute-start(bf16[384,1536]{1,0:T(8,128)(2,1)S(1)} %fusion.2), channel_id=1, source_target_pairs={{0,1},{1,0},{2,3},{3,2},{4,5},{5,4},{6,7},{7,6},{8,9},{9,8},{10,11... | collective-permute-start | bytes 3538952 | tf_op jit(solution)/shard_map/ppermute | solution.py:630
  114.8 12.0 %collective-permute-start.2 = (f32[32,768]{1,0:T(8,128)S(1)}, f32[32,768]{1,0:T(8,128)S(1)}, u32[]{:S(2)}, u32[]{:S(2)}) collective-permute-start(f32[32,768]{1,0:T(8,128)S(1)} %add.270), channel_id=1, source_target_pairs={{0,1},{1,0},{2,3},{3,2},{4,5},{5,4},{6,7},{7,6},{8,9},{9,8},{10,11... | collective-permute-start | bytes 294920 | tf_op jit(solution)/shard_map/ppermute | solution.py:630
  130.3 22.6 %collective-permute-start.40 = (bf16[768,768]{1,0:T(8,128)(2,1)S(1)}, bf16[768,768]{1,0:T(8,128)(2,1)S(1)}, u32[]{:S(2)}, u32[]{:S(2)}) collective-permute-start(bf16[768,768]{1,0:T(8,128)(2,1)S(1)} %fusion.3), channel_id=1, source_target_pairs={{0,1},{1,0},{2,3},{3,2},{4,5},{5,4},{6,7},{7,6},{8,9},{9,8},{10,11... | collective-permute-start | bytes 3538952 | tf_op jit(solution)/shard_map/ppermute | solution.py:630
  133.5 41.4 %collective-permute-start.8 = (bf16[384,1920]{1,0:T(8,128)(2,1)S(1)}, bf16[384,1920]{1,0:T(8,128)(2,1)S(1)}, u32[]{:S(2)}, u32[]{:S(2)}) collective-permute-start(bf16[384,1920]{1,0:T(8,128)(2,1)S(1)} %fusion), channel_id=1, source_target_pairs={{0,1},{1,0},{2,3},{3,2},{4,5},{5,4},{6,7},{7,6},{8,9},{9,8},{10,11... | collective-permute-start | bytes 4423688 | tf_op jit(solution)/shard_map/ppermute | solution.py:630
  134.4 19.0 %collective-permute-start.25 = (bf16[192,1536]{1,0:T(8,128)(2,1)S(1)}, bf16[192,1536]{1,0:T(8,128)(2,1)S(1)}, u32[]{:S(2)}, u32[]{:S(2)}) collective-permute-start(bf16[192,1536]{1,0:T(8,128)(2,1)S(1)} %fusion.7), channel_id=1, source_target_pairs={{0,2},{1,3},{2,0},{3,1},{4,6},{5,7},{6,4},{7,5},{8,10},{9,11},{10,... | collective-permute-start | bytes 1769480 | tf_op jit(solution)/shard_map/ppermute | solution.py:633
  134.8 69.1 %collective-permute-start.6 = (f32[32,768]{1,0:T(8,128)S(1)}, f32[32,768]{1,0:T(8,128)S(1)}, u32[]{:S(2)}, u32[]{:S(2)}) collective-permute-start(f32[32,768]{1,0:T(8,128)S(1)} %add.272), channel_id=1, source_target_pairs={{0,12},{1,13},{2,14},{3,15},{4,0},{5,1},{6,2},{7,3},{8,4},{9,5},{1... | collective-permute-start | bytes 294920 | tf_op jit(solution)/shard_map/ppermute | solution.py:636
  153.1 31.1 %collective-permute-start.41 = (bf16[384,768]{1,0:T(8,128)(2,1)S(1)}, bf16[384,768]{1,0:T(8,128)(2,1)S(1)}, u32[]{:S(2)}, u32[]{:S(2)}) collective-permute-start(bf16[384,768]{1,0:T(8,128)(2,1)S(1)} %fusion.8), channel_id=1, source_target_pairs={{0,2},{1,3},{2,0},{3,1},{4,6},{5,7},{6,4},{7,5},{8,10},{9,11},{10,... | collective-permute-start | bytes 1769480 | tf_op jit(solution)/shard_map/ppermute | solution.py:633
  153.8 23.0 %collective-permute-start.28 = (bf16[48,1536]{1,0:T(8,128)(2,1)S(1)}, bf16[48,1536]{1,0:T(8,128)(2,1)S(1)}, u32[]{:S(2)}, u32[]{:S(2)}) collective-permute-start(bf16[48,1536]{1,0:T(8,128)(2,1)S(1)} %get-tuple-element.114), channel_id=1, source_target_pairs={{0,12},{1,13},{2,14},{3,15},{4,0},{5,1},{6,2},{7,3},{8,4},{9,5},{1... | collective-permute-start | bytes 442376 | tf_op jit(solution)/shard_map/ppermute | solution.py:636
  158.0 19.7 %collective-permute-start.27 = (bf16[48,1536]{1,0:T(8,128)(2,1)S(1)}, bf16[48,1536]{1,0:T(8,128)(2,1)S(1)}, u32[]{:S(2)}, u32[]{:S(2)}) collective-permute-start(bf16[48,1536]{1,0:T(8,128)(2,1)S(1)} %get-tuple-element.115), channel_id=1, source_target_pairs={{0,8},{1,9},{2,10},{3,11},{4,12},{5,13},{6,14},{7,15},{8,0},{9,1},... | collective-permute-start | bytes 442376 | tf_op jit(solution)/shard_map/ppermute | solution.py:636
  176.8 26.7 %collective-permute-start.9 = (bf16[192,1920]{1,0:T(8,128)(2,1)S(1)}, bf16[192,1920]{1,0:T(8,128)(2,1)S(1)}, u32[]{:S(2)}, u32[]{:S(2)}) collective-permute-start(bf16[192,1920]{1,0:T(8,128)(2,1)S(1)} %fusion.6), channel_id=1, source_target_pairs={{0,2},{1,3},{2,0},{3,1},{4,6},{5,7},{6,4},{7,5},{8,10},{9,11},{10,... | collective-permute-start | bytes 2211848 | tf_op jit(solution)/shard_map/ppermute | solution.py:633
  184.2 13.9 %collective-permute-start.30 = (bf16[48,1536]{1,0:T(8,128)(2,1)S(1)}, bf16[48,1536]{1,0:T(8,128)(2,1)S(1)}, u32[]{:S(2)}, u32[]{:S(2)}) collective-permute-start(bf16[48,1536]{1,0:T(8,128)(2,1)S(1)} %fusion.17), channel_id=1, source_target_pairs={{0,8},{1,9},{2,10},{3,11},{4,12},{5,13},{6,14},{7,15},{8,0},{9,1},... | collective-permute-start | bytes 442376 | tf_op jit(solution)/shard_map/ppermute | solution.py:636
  184.2 13.9 %collective-permute-start.29 = (bf16[48,1536]{1,0:T(8,128)(2,1)S(1)}, bf16[48,1536]{1,0:T(8,128)(2,1)S(1)}, u32[]{:S(2)}, u32[]{:S(2)}) collective-permute-start(bf16[48,1536]{1,0:T(8,128)(2,1)S(1)} %fusion.17), channel_id=1, source_target_pairs={{0,4},{1,5},{2,6},{3,7},{4,8},{5,9},{6,10},{7,11},{8,12},{9,13},{1... | collective-permute-start | bytes 442376 | tf_op jit(solution)/shard_map/ppermute | solution.py:636
  189.7 14.9 %collective-permute-start.5 = (f32[32,768]{1,0:T(8,128)S(1)}, f32[32,768]{1,0:T(8,128)S(1)}, u32[]{:S(2)}, u32[]{:S(2)}) collective-permute-start(f32[32,768]{1,0:T(8,128)S(1)} %add.272), channel_id=1, source_target_pairs={{0,8},{1,9},{2,10},{3,11},{4,12},{5,13},{6,14},{7,15},{8,0},{9,1},... | collective-permute-start | bytes 294920 | tf_op jit(solution)/shard_map/ppermute | solution.py:636
  198.1 19.9 %collective-permute-start.43 = (bf16[96,768]{1,0:T(8,128)(2,1)S(1)}, bf16[96,768]{1,0:T(8,128)(2,1)S(1)}, u32[]{:S(2)}, u32[]{:S(2)}) collective-permute-start(bf16[96,768]{1,0:T(8,128)(2,1)S(1)} %get-tuple-element.112), channel_id=1, source_target_pairs={{0,8},{1,9},{2,10},{3,11},{4,12},{5,13},{6,14},{7,15},{8,0},{9,1},... | collective-permute-start | bytes 442376 | tf_op jit(solution)/shard_map/ppermute | solution.py:636
  203.5 14.5 %collective-permute-start.42 = (bf16[96,768]{1,0:T(8,128)(2,1)S(1)}, bf16[96,768]{1,0:T(8,128)(2,1)S(1)}, u32[]{:S(2)}, u32[]{:S(2)}) collective-permute-start(bf16[96,768]{1,0:T(8,128)(2,1)S(1)} %get-tuple-element.110), channel_id=1, source_target_pairs={{0,4},{1,5},{2,6},{3,7},{4,8},{5,9},{6,10},{7,11},{8,12},{9,13},{1... | collective-permute-start | bytes 442376 | tf_op jit(solution)/shard_map/ppermute | solution.py:636
  204.0 14.1 %collective-permute-start.4 = (f32[32,768]{1,0:T(8,128)S(1)}, f32[32,768]{1,0:T(8,128)}, u32[]{:S(2)}, u32[]{:S(2)}) collective-permute-start(f32[32,768]{1,0:T(8,128)S(1)} %add.272), channel_id=1, source_target_pairs={{0,4},{1,5},{2,6},{3,7},{4,8},{5,9},{6,10},{7,11},{8,12},{9,13},{1... | collective-permute-start | bytes 294920 | tf_op jit(solution)/shard_map/ppermute | solution.py:636
  204.6 42.2 %collective-permute-start.32 = (bf16[192,1536]{1,0:T(8,128)(2,1)S(1)}, bf16[192,1536]{1,0:T(8,128)(2,1)S(1)}, u32[]{:S(2)}, u32[]{:S(2)}) collective-permute-start(bf16[192,1536]{1,0:T(8,128)(2,1)S(1)} %pad_maximum_fusion.1.refs_0_), channel_id=1, source_target_pairs={{0,2},{1,3},{2,0},{3,1},{4,6},{5,7},{6,4},{7,5},{8,10},{9,11},{10,... | collective-permute-start | bytes 1769480 | tf_op jit(solution)/shard_map/ppermute | solution.py:633
  206.1 16.6 %collective-permute-start.12 = (bf16[48,1920]{1,0:T(8,128)(2,1)S(1)}, bf16[48,1920]{1,0:T(8,128)(2,1)S(1)}, u32[]{:S(2)}, u32[]{:S(2)}) collective-permute-start(bf16[48,1920]{1,0:T(8,128)(2,1)S(1)} %get-tuple-element.108), channel_id=1, source_target_pairs={{0,12},{1,13},{2,14},{3,15},{4,0},{5,1},{6,2},{7,3},{8,4},{9,5},{1... | collective-permute-start | bytes 552968 | tf_op jit(solution)/shard_map/ppermute | solution.py:636
  218.0 15.9 %collective-permute-start.11 = (bf16[48,1920]{1,0:T(8,128)(2,1)S(1)}, bf16[48,1920]{1,0:T(8,128)(2,1)S(1)}, u32[]{:S(2)}, u32[]{:S(2)}) collective-permute-start(bf16[48,1920]{1,0:T(8,128)(2,1)S(1)} %get-tuple-element.109), channel_id=1, source_target_pairs={{0,8},{1,9},{2,10},{3,11},{4,12},{5,13},{6,14},{7,15},{8,0},{9,1},... | collective-permute-start | bytes 552968 | tf_op jit(solution)/shard_map/ppermute | solution.py:636
  218.0 15.9 %collective-permute-start.10 = (bf16[48,1920]{1,0:T(8,128)(2,1)S(1)}, bf16[48,1920]{1,0:T(8,128)(2,1)S(1)}, u32[]{:S(2)}, u32[]{:S(2)}) collective-permute-start(bf16[48,1920]{1,0:T(8,128)(2,1)S(1)} %get-tuple-element.107), channel_id=1, source_target_pairs={{0,4},{1,5},{2,6},{3,7},{4,8},{5,9},{6,10},{7,11},{8,12},{9,13},{1... | collective-permute-start | bytes 552968 | tf_op jit(solution)/shard_map/ppermute | solution.py:636
  218.1 17.0 %collective-permute-start.47 = (bf16[96,768]{1,0:T(8,128)(2,1)S(1)}, bf16[96,768]{1,0:T(8,128)(2,1)S(1)}, u32[]{:S(2)}, u32[]{:S(2)}) collective-permute-start(bf16[96,768]{1,0:T(8,128)(2,1)S(1)} %fusion.14), channel_id=1, source_target_pairs={{0,12},{1,13},{2,14},{3,15},{4,0},{5,1},{6,2},{7,3},{8,4},{9,5},{1... | collective-permute-start | bytes 442376 | tf_op jit(solution)/shard_map/ppermute | solution.py:636
  222.7 24.1 %collective-permute-start.46 = (bf16[96,768]{1,0:T(8,128)(2,1)S(1)}, bf16[96,768]{1,0:T(8,128)(2,1)S(1)}, u32[]{:S(2)}, u32[]{:S(2)}) collective-permute-start(bf16[96,768]{1,0:T(8,128)(2,1)S(1)} %fusion.14), channel_id=1, source_target_pairs={{0,8},{1,9},{2,10},{3,11},{4,12},{5,13},{6,14},{7,15},{8,0},{9,1},... | collective-permute-start | bytes 442376 | tf_op jit(solution)/shard_map/ppermute | solution.py:636
  233.8 12.9 %collective-permute-start.45 = (bf16[96,768]{1,0:T(8,128)(2,1)S(1)}, bf16[96,768]{1,0:T(8,128)(2,1)S(1)}, u32[]{:S(2)}, u32[]{:S(2)}) collective-permute-start(bf16[96,768]{1,0:T(8,128)(2,1)S(1)} %fusion.14), channel_id=1, source_target_pairs={{0,4},{1,5},{2,6},{3,7},{4,8},{5,9},{6,10},{7,11},{8,12},{9,13},{1... | collective-permute-start | bytes 442376 | tf_op jit(solution)/shard_map/ppermute | solution.py:636
  233.8 25.9 %collective-permute-start.33 = (bf16[192,1536]{1,0:T(8,128)(2,1)S(1)}, bf16[192,1536]{1,0:T(8,128)(2,1)S(1)}, u32[]{:S(2)}, u32[]{:S(2)}) collective-permute-start(bf16[192,1536]{1,0:T(8,128)(2,1)S(1)} %pad_maximum_fusion.1.refs_0_), channel_id=1, source_target_pairs={{0,1},{1,0},{2,3},{3,2},{4,5},{5,4},{6,7},{7,6},{8,9},{9,8},{10,11... | collective-permute-start | bytes 1769480 | tf_op jit(solution)/shard_map/ppermute | solution.py:630
  235.1 14.4 %collective-permute-start.15 = (bf16[48,1920]{1,0:T(8,128)(2,1)S(1)}, bf16[48,1920]{1,0:T(8,128)(2,1)S(1)}, u32[]{:S(2)}, u32[]{:S(2)}) collective-permute-start(bf16[48,1920]{1,0:T(8,128)(2,1)S(1)} %fusion.11), channel_id=1, source_target_pairs={{0,12},{1,13},{2,14},{3,15},{4,0},{5,1},{6,2},{7,3},{8,4},{9,5},{1... | collective-permute-start | bytes 552968 | tf_op jit(solution)/shard_map/ppermute | solution.py:636
  246.7 11.9 %collective-permute-start.14 = (bf16[48,1920]{1,0:T(8,128)(2,1)S(1)}, bf16[48,1920]{1,0:T(8,128)(2,1)S(1)}, u32[]{:S(2)}, u32[]{:S(2)}) collective-permute-start(bf16[48,1920]{1,0:T(8,128)(2,1)S(1)} %fusion.11), channel_id=1, source_target_pairs={{0,8},{1,9},{2,10},{3,11},{4,12},{5,13},{6,14},{7,15},{8,0},{9,1},... | collective-permute-start | bytes 552968 | tf_op jit(solution)/shard_map/ppermute | solution.py:636
  246.7 14.3 %collective-permute-start.35 = (bf16[192,1536]{1,0:T(8,128)(2,1)S(1)}, bf16[192,1536]{1,0:T(8,128)(2,1)S(1)}, u32[]{:S(2)}, u32[]{:S(2)}) collective-permute-start(bf16[192,1536]{1,0:T(8,128)(2,1)S(1)} %pad_maximum_fusion.1.refs_0_), channel_id=1, source_target_pairs={{0,16},{1,17},{2,18},{3,19},{4,20},{5,21},{6,22},{7,23},{8,24},{9,... | collective-permute-start | bytes 1769480 | tf_op jit(solution)/shard_map/ppermute | solution.py:627
  246.8 12.9 %collective-permute-start.13 = (bf16[48,1920]{1,0:T(8,128)(2,1)S(1)}, bf16[48,1920]{1,0:T(8,128)(2,1)S(1)}, u32[]{:S(2)}, u32[]{:S(2)}) collective-permute-start(bf16[48,1920]{1,0:T(8,128)(2,1)S(1)} %fusion.11), channel_id=1, source_target_pairs={{0,4},{1,5},{2,6},{3,7},{4,8},{5,9},{6,10},{7,11},{8,12},{9,13},{1... | collective-permute-start | bytes 552968 | tf_op jit(solution)/shard_map/ppermute | solution.py:636
  249.5 12.7 %collective-permute-start.48 = (bf16[384,768]{1,0:T(8,128)(2,1)S(1)}, bf16[384,768]{1,0:T(8,128)(2,1)S(1)}, u32[]{:S(2)}, u32[]{:S(2)}) collective-permute-start(bf16[384,768]{1,0:T(8,128)(2,1)S(1)} %pad_maximum_fusion.2.refs_0_), channel_id=1, source_target_pairs={{0,2},{1,3},{2,0},{3,1},{4,6},{5,7},{6,4},{7,5},{8,10},{9,11},{10,... | collective-permute-start | bytes 1769480 | tf_op jit(solution)/shard_map/ppermute | solution.py:633
  258.6 15.5 %collective-permute-start.49 = (bf16[384,768]{1,0:T(8,128)(2,1)S(1)}, bf16[384,768]{1,0:T(8,128)(2,1)S(1)}, u32[]{:S(2)}, u32[]{:S(2)}) collective-permute-start(bf16[384,768]{1,0:T(8,128)(2,1)S(1)} %pad_maximum_fusion.2.refs_0_), channel_id=1, source_target_pairs={{0,1},{1,0},{2,3},{3,2},{4,5},{5,4},{6,7},{7,6},{8,9},{9,8},{10,11... | collective-permute-start | bytes 1769480 | tf_op jit(solution)/shard_map/ppermute | solution.py:630
  259.7 14.4 %collective-permute-start.51 = (bf16[384,768]{1,0:T(8,128)(2,1)S(1)}, bf16[384,768]{1,0:T(8,128)(2,1)S(1)}, u32[]{:S(2)}, u32[]{:S(2)}) collective-permute-start(bf16[384,768]{1,0:T(8,128)(2,1)S(1)} %pad_maximum_fusion.2.refs_0_), channel_id=1, source_target_pairs={{0,16},{1,17},{2,18},{3,19},{4,20},{5,21},{6,22},{7,23},{8,24},{9,... | collective-permute-start | bytes 1769480 | tf_op jit(solution)/shard_map/ppermute | solution.py:627
  259.8 24.0 %collective-permute-start.16 = (bf16[192,1920]{1,0:T(8,128)(2,1)S(1)}, bf16[192,1920]{1,0:T(8,128)(2,1)S(1)}, u32[]{:S(2)}, u32[]{:S(2)}) collective-permute-start(bf16[192,1920]{1,0:T(8,128)(2,1)S(1)} %pad_maximum_fusion.refs_0_), channel_id=1, source_target_pairs={{0,2},{1,3},{2,0},{3,1},{4,6},{5,7},{6,4},{7,5},{8,10},{9,11},{10,... | collective-permute-start | bytes 2211848 | tf_op jit(solution)/shard_map/ppermute | solution.py:633
  261.0 21.7 %collective-permute-start.34 = (bf16[192,1536]{1,0:T(8,128)(2,1)S(1)}, bf16[192,1536]{1,0:T(8,128)(2,1)S(1)}, u32[]{:S(2)}, u32[]{:S(2)}) collective-permute-start(bf16[192,1536]{1,0:T(8,128)(2,1)S(1)} %collective-permute-done.32.refs_1_), channel_id=1, source_target_pairs={{0,1},{1,0},{2,3},{3,2},{4,5},{5,4},{6,7},{7,6},{8,9},{9,8},{10,11... | collective-permute-start | bytes 1769480 | tf_op jit(solution)/shard_map/ppermute | solution.py:630
  262.2 22.6 %collective-permute-start.36 = (bf16[192,1536]{1,0:T(8,128)(2,1)S(1)}, bf16[192,1536]{1,0:T(8,128)(2,1)S(1)}, u32[]{:S(2)}, u32[]{:S(2)}) collective-permute-start(bf16[192,1536]{1,0:T(8,128)(2,1)S(1)} %collective-permute-done.32.refs_1_), channel_id=1, source_target_pairs={{0,16},{1,17},{2,18},{3,19},{4,20},{5,21},{6,22},{7,23},{8,24},{9,... | collective-permute-start | bytes 1769480 | tf_op jit(solution)/shard_map/ppermute | solution.py:627
  274.1 10.7 %collective-permute-start.37 = (bf16[192,1536]{1,0:T(8,128)(2,1)S(1)}, bf16[192,1536]{1,0:T(8,128)(2,1)S(1)}, u32[]{:S(2)}, u32[]{:S(2)}) collective-permute-start(bf16[192,1536]{1,0:T(8,128)(2,1)S(1)} %collective-permute-done.33.refs_2_), channel_id=1, source_target_pairs={{0,16},{1,17},{2,18},{3,19},{4,20},{5,21},{6,22},{7,23},{8,24},{9,... | collective-permute-start | bytes 1769480 | tf_op jit(solution)/shard_map/ppermute | solution.py:627
  274.1 15.0 %collective-permute-start.50 = (bf16[384,768]{1,0:T(8,128)(2,1)S(1)}, bf16[384,768]{1,0:T(8,128)(2,1)}, u32[]{:S(2)}, u32[]{:S(2)}) collective-permute-start(bf16[384,768]{1,0:T(8,128)(2,1)S(1)} %collective-permute-done.48.refs_1_), channel_id=1, source_target_pairs={{0,1},{1,0},{2,3},{3,2},{4,5},{5,4},{6,7},{7,6},{8,9},{9,8},{10,11... | collective-permute-start | bytes 1769480 | tf_op jit(solution)/shard_map/ppermute | solution.py:630
  282.7 14.2 %collective-permute-start.17 = (bf16[192,1920]{1,0:T(8,128)(2,1)S(1)}, bf16[192,1920]{1,0:T(8,128)(2,1)S(1)}, u32[]{:S(2)}, u32[]{:S(2)}) collective-permute-start(bf16[192,1920]{1,0:T(8,128)(2,1)S(1)} %pad_maximum_fusion.refs_0_), channel_id=1, source_target_pairs={{0,1},{1,0},{2,3},{3,2},{4,5},{5,4},{6,7},{7,6},{8,9},{9,8},{10,11... | collective-permute-start | bytes 2211848 | tf_op jit(solution)/shard_map/ppermute | solution.py:630
  283.8 21.1 %collective-permute-start.18 = (bf16[192,1920]{1,0:T(8,128)(2,1)S(1)}, bf16[192,1920]{1,0:T(8,128)(2,1)S(1)}, u32[]{:S(2)}, u32[]{:S(2)}) collective-permute-start(bf16[192,1920]{1,0:T(8,128)(2,1)S(1)} %collective-permute-done.16.refs_1_), channel_id=1, source_target_pairs={{0,1},{1,0},{2,3},{3,2},{4,5},{5,4},{6,7},{7,6},{8,9},{9,8},{10,11... | collective-permute-start | bytes 2211848 | tf_op jit(solution)/shard_map/ppermute | solution.py:630
  289.2 15.7 %collective-permute-start.38 = (bf16[192,1536]{1,0:T(8,128)(2,1)S(1)}, bf16[192,1536]{1,0:T(8,128)(2,1)S(1)}, u32[]{:S(2)}, u32[]{:S(2)}) collective-permute-start(bf16[192,1536]{1,0:T(8,128)(2,1)S(1)} %collective-permute-done.34.refs_3_), channel_id=1, source_target_pairs={{0,16},{1,17},{2,18},{3,19},{4,20},{5,21},{6,22},{7,23},{8,24},{9,... | collective-permute-start | bytes 1769480 | tf_op jit(solution)/shard_map/ppermute | solution.py:627
  289.2 38.8 %collective-permute-start.19 = (bf16[192,1920]{1,0:T(8,128)(2,1)S(1)}, bf16[192,1920]{1,0:T(8,128)(2,1)}, u32[]{:S(2)}, u32[]{:S(2)}) collective-permute-start(bf16[192,1920]{1,0:T(8,128)(2,1)S(1)} %pad_maximum_fusion.refs_0_), channel_id=1, source_target_pairs={{0,16},{1,17},{2,18},{3,19},{4,20},{5,21},{6,22},{7,23},{8,24},{9,... | collective-permute-start | bytes 2211848 | tf_op jit(solution)/shard_map/ppermute | solution.py:627
  289.7 38.3 %collective-permute-start.20 = (bf16[192,1920]{1,0:T(8,128)(2,1)S(1)}, bf16[192,1920]{1,0:T(8,128)(2,1)}, u32[]{:S(2)}, u32[]{:S(2)}) collective-permute-start(bf16[192,1920]{1,0:T(8,128)(2,1)S(1)} %collective-permute-done.16.refs_1_), channel_id=1, source_target_pairs={{0,16},{1,17},{2,18},{3,19},{4,20},{5,21},{6,22},{7,23},{8,24},{9,... | collective-permute-start | bytes 2211848 | tf_op jit(solution)/shard_map/ppermute | solution.py:627
  297.0 31.0 %collective-permute-start.21 = (bf16[192,1920]{1,0:T(8,128)(2,1)S(1)}, bf16[192,1920]{1,0:T(8,128)(2,1)}, u32[]{:S(2)}, u32[]{:S(2)}) collective-permute-start(bf16[192,1920]{1,0:T(8,128)(2,1)S(1)} %collective-permute-done.17.refs_2_), channel_id=1, source_target_pairs={{0,16},{1,17},{2,18},{3,19},{4,20},{5,21},{6,22},{7,23},{8,24},{9,... | collective-permute-start | bytes 2211848 | tf_op jit(solution)/shard_map/ppermute | solution.py:627
  304.9 23.1 %collective-permute-start.22 = (bf16[192,1920]{1,0:T(8,128)(2,1)S(1)}, bf16[192,1920]{1,0:T(8,128)(2,1)}, u32[]{:S(2)}, u32[]{:S(2)}) collective-permute-start(bf16[192,1920]{1,0:T(8,128)(2,1)S(1)} %collective-permute-done.18.refs_3_), channel_id=1, source_target_pairs={{0,16},{1,17},{2,18},{3,19},{4,20},{5,21},{6,22},{7,23},{8,24},{9,... | collective-permute-start | bytes 2211848 | tf_op jit(solution)/shard_map/ppermute | solution.py:627
  306.0 14.1 %collective-permute-start.54 = (bf16[384,768]{1,0:T(8,128)(2,1)}, bf16[384,768]{1,0:T(8,128)(2,1)}, u32[]{:S(2)}, u32[]{:S(2)}) collective-permute-start(bf16[384,768]{1,0:T(8,128)(2,1)} %collective-permute-done.50.refs_3_), channel_id=1, source_target_pairs={{0,16},{1,17},{2,18},{3,19},{4,20},{5,21},{6,22},{7,23},{8,24},{9,... | collective-permute-start | bytes 1769480 | tf_op jit(solution)/shard_map/ppermute | solution.py:627
  (35 other events, 890.5 us)
where the time goes:
time: 344 us; the launch traced here: 343 us
  waiting for transfers between devices  119 us (35%)
  Pallas kernels  110 us (32%)
  starting transfers between devices  70.3 us (20%)
  local copies, waits for them, and re-layouts  34.9 us (10%)
  other arithmetic  8.54 us (2%)
    ppermute x10, waiting for transfers between devices, first(): lax.ppermute(v, AXES, self.pairs(lambda c, b: (c, b ^ (1 if c == 0 else 2...  76.2 us
    ppermute x21, starting transfers between devices, along(): lax.ppermute(v, AXES, self.pairs(lambda c, b: (c, (b + 4 * k) % self.nb)))  44.7 us
    ppermute x21, waiting for transfers between devices, along(): lax.ppermute(v, AXES, self.pairs(lambda c, b: (c, (b + 4 * k) % self.nb)))  40.6 us
    pallas_call x3, Pallas kernels, place(): pl.pallas_call(functools.partial(place_kernel, links.nz, widths), out_sha...  24.6 us
    pallas_call x1, Pallas kernels, front(): pl.pallas_call(front_kernel, out_shape=shapes, in_specs=[smem()] * 3 + [v...  20.8 us
    pallas_call x1, Pallas kernels, tail(): pl.pallas_call(tail_kernel, out_shape=[jax.ShapeDtypeStruct((D, 1920), BF...  18.2 us
    pallas_call x1, Pallas kernels, attend_back(): pl.pallas_call(attend_back_kernel, out_shape=[jax.ShapeDtypeStruct((rows,...  17.3 us
    ppermute x10, starting transfers between devices, first(): lax.ppermute(v, AXES, self.pairs(lambda c, b: (c, b ^ (1 if c == 0 else 2...  14.6 us
  transfers between devices with their start and end apart: 55, of which 19 were waited for; matrix products, arithmetic and copies ran while one was open for 10% of the time, Pallas kernels for 25%

commit v1 on v0

v1 whole, which is shorter than its diff:
```python
import functools

import jax
import jax.numpy as jnp
from jax import lax
from jax.experimental import pallas as pl
from jax.experimental.pallas import tpu as pltpu
from jax.sharding import PartitionSpec as P

F32 = jnp.float32
BF16 = jnp.bfloat16
HEADS = 12
HEAD_DIM = 64
SEQ = 256
ROWS = 128
MICRO = 2
SRC = 4
D = 768
FF = 3072
OUT = 81
EPSILON = 1e-05
NEGATIVE = -1e30
AXES = ("mod", "batch")

G1, S1, BQ, BV, BAO, G2, S2, BFO, SB, BFI = range(10)
SMALL_ROWS = 32
REL_ROW = 16


def dot(a, b):
    return lax.dot_general(a, b, (((1,), (0,)), ((), ())), preferred_element_type=F32)


def dot_nt(a, b):
    return lax.dot_general(a, b, (((1,), (1,)), ((), ())), preferred_element_type=F32)


def dot_tn(a, b):
    return lax.dot_general(a, b, (((0,), (0,)), ((), ())), preferred_element_type=F32)


def iota(shape, axis):
    return lax.broadcasted_iota(jnp.int32, shape, axis)


def aligned(start, size):
    return pl.ds(pl.multiple_of(start, size), size)


def normalise(values):
    centred = values - jnp.mean(values, axis=-1, keepdims=True)
    inverse = lax.rsqrt(jnp.mean(centred * centred, axis=-1, keepdims=True) + EPSILON)
    return centred * inverse, inverse


def norm_back(grad, normed, inverse, gain):
    scaled = grad * gain
    mean_grad = jnp.mean(scaled, axis=-1, keepdims=True)
    along = jnp.mean(scaled * normed, axis=-1, keepdims=True)
    return inverse * (scaled - mean_grad - normed * along)


def head_masks():
    lane = iota((1, 2 * HEAD_DIM), 1)
    low = (lane < HEAD_DIM).astype(F32).astype(BF16)
    return low, (1.0 - low.astype(F32)).astype(BF16)


def route_of(routes_ref, d, m, j):
    route = routes_ref[m, 0, d, j]
    return route // SRC, route % SRC


def onehot_vocab(ids_ref, m, block):
    row_ids = ids_ref[m : m + 1, aligned(block * ROWS, ROWS)]
    return (iota((ROWS, ROWS), 0) == row_ids).astype(F32).astype(BF16)


def front_kernel(
    here_ref, routes_ref, lengths_ref,
    feats_ref, ids_ref, bucket_ref, rel_ref, proj_ref, table_ref,
    g1_ref, s1_ref, bqv_ref, bao_ref, g2_ref, s2_ref, bfo_ref, sb_ref, bfi_ref,
    wqkv_hbm, wao_hbm,
    x_ref, h1_ref, qkv_ref, pt_ref, ctx_ref, mid_ref, h2_ref, vec_ref, row_ref,
    wqkv, wao, sems, bias, mask, frow, tab,
):
    d = here_ref[0]
    copy_qkv = pltpu.make_async_copy(wqkv_hbm, wqkv, sems.at[0])
    copy_ao = pltpu.make_async_copy(wao_hbm, wao, sems.at[1])
    copy_qkv.start()
    copy_ao.start()
    vocab = table_ref.shape[0]
    tab[...] = jnp.zeros_like(tab)
    tab[:vocab, :] = table_ref[...]
    vec_ref[...] = jnp.zeros_like(vec_ref)
    for at, ref in (
        (G1, g1_ref), (S1, s1_ref), (BAO, bao_ref), (G2, g2_ref), (S2, s2_ref), (BFO, bfo_ref), (SB, sb_ref)
    ):
        vec_ref[at : at + 1, :] = ref[...].astype(F32).reshape(1, D)
    vec_ref[BQ : BV + 1, :] = bqv_ref[...].astype(F32)
    for i in range(FF // D):
        vec_ref[BFI + i : BFI + i + 1, :] = bfi_ref[i * D : (i + 1) * D].astype(F32).reshape(1, D)
    line = jnp.concatenate([bucket_ref[...].reshape(1, 2 * SEQ - 1), jnp.zeros((1, 1), jnp.int32)], axis=1)
    row_ref[...] = pltpu.roll(line, SEQ + 1, 1)
    for m in range(MICRO):
        for j in range(2):
            modality, block = route_of(routes_ref, d, m, j)
            rows = slice((m * 2 + j) * ROWS, (m * 2 + j + 1) * ROWS)

            @pl.when(modality == 0)
            def _(m=m, block=block, rows=rows):
                feats = feats_ref[m, aligned(block * ROWS, ROWS), :]
                spoken = dot(feats, proj_ref[...]) + vec_ref[SB : SB + 1, :]
                x_ref[rows, :] = spoken.astype(BF16)

            @pl.when(modality != 0)
            def _(m=m, block=block, rows=rows):
                hot = onehot_vocab(ids_ref, m, block)
                x_ref[rows, :] = dot_tn(hot, tab[...]).astype(BF16)

    hot = (iota((rel_ref.shape[1], 2 * SEQ), 0) == row_ref[...]).astype(F32).astype(BF16)
    frow[0:HEADS, :] = dot(rel_ref[...], hot)

    def make_bias(h, _):
        base = jnp.broadcast_to(frow[pl.ds(h, 1), :], (16, 2 * SEQ))
        base = pltpu.roll(base, 0, 1, stride=1, stride_axis=0)
        for a in range(SEQ // 16):
            shifted = pltpu.roll(base, 16 * a, 1) if a else base
            bias[h, 16 * a : 16 * a + 16, :] = shifted[:, :SEQ].astype(BF16)
        return 0

    lax.fori_loop(0, HEADS, make_bias, 0)
    at_j = iota((SEQ, SEQ), 0)
    at_i = iota((SEQ, SEQ), 1)
    for m in range(MICRO):
        modality, _ = route_of(routes_ref, d, m, 0)
        first = lengths_ref[m, 0, d, 0]
        second = lengths_ref[m, 0, d, 1]
        whole = jnp.where(at_j < first + second, 0.0, NEGATIVE)
        limit = jnp.where(at_j < ROWS, first, second + ROWS)
        same = (at_j // ROWS) == (at_i // ROWS)
        halves = jnp.where(same, jnp.where(at_j < limit, 0.0, NEGATIVE), NEGATIVE)
        mask[m] = jnp.where(modality == 0, whole, halves)

    def first_norm(r, _):
        rows = aligned(r * ROWS, ROWS)
        normed, _ = normalise(x_ref[rows, :].astype(F32))
        h1_ref[rows, :] = (normed * vec_ref[G1 : G1 + 1, :] + vec_ref[S1 : S1 + 1, :]).astype(BF16)
        return 0

    lax.fori_loop(0, MICRO * SEQ // ROWS, first_norm, 0)
    copy_qkv.wait()
    for n in range(9):
        cols = slice(n * 256, (n + 1) * 256)
        part = dot(h1_ref[...], wqkv[:, cols])
        if n < 3:
            part = part + vec_ref[BQ : BQ + 1, cols]
        elif n >= 6:
            part = part + vec_ref[BV : BV + 1, (n - 6) * 256 : (n - 5) * 256]
        qkv_ref[:, cols] = part.astype(BF16)

    low, high = head_masks()

    def attention(step, _):
        m = step // (HEADS // 2)
        pair = step - m * (HEADS // 2)
        rows = aligned(m * SEQ, SEQ)
        q = qkv_ref[rows, aligned(pair * 128, 128)]
        k = qkv_ref[rows, aligned(D + pair * 128, 128)]
        v = qkv_ref[rows, aligned(2 * D + pair * 128, 128)]
        total = jnp.zeros((SEQ, 128), F32)
        for s, keep in enumerate((low, high)):
            scores = dot_nt(k * keep, q) * HEAD_DIM ** (-0.5)
            scores = scores + bias[2 * pair + s].astype(F32) + mask[m]
            weights = jnp.exp(scores - jnp.max(scores, axis=0, keepdims=True))
            weights = weights * (1.0 / jnp.sum(weights, axis=0, keepdims=True))
            weights = weights.astype(BF16)
            pt_ref[m * HEADS + 2 * pair + s] = weights
            total = total + dot_tn(weights, v * keep)
        ctx_ref[rows, aligned(pair * 128, 128)] = total.astype(BF16)
        return 0

    lax.fori_loop(0, MICRO * HEADS // 2, attention, 0)
    copy_ao.wait()
    for n in range(3):
        cols = slice(n * 256, (n + 1) * 256)
        mid_ref[:, cols] = (
            x_ref[:, cols].astype(F32) + dot(ctx_ref[...], wao[:, cols]) + vec_ref[BAO : BAO + 1, cols]
        )

    def second_norm(r, _):
        rows = aligned(r * ROWS, ROWS)
        normed, _ = normalise(mid_ref[rows, :])
        h2_ref[rows, :] = (normed * vec_ref[G2 : G2 + 1, :] + vec_ref[S2 : S2 + 1, :]).astype(BF16)
        return 0

    lax.fori_loop(0, MICRO * SEQ // ROWS, second_norm, 0)


def resident(*values):
    return [pltpu.with_memory_space_constraint(v, pltpu.VMEM) for v in values]


def in_hbm(*values):
    return [pltpu.with_memory_space_constraint(v, pltpu.HBM) for v in values]


def in_vmem(shape, dtype):
    return pltpu.VMEM(shape, dtype)


def smem():
    return pl.BlockSpec(memory_space=pltpu.SMEM)


def hbm():
    return pl.BlockSpec(memory_space=pl.ANY)


def vmem():
    return pl.BlockSpec(memory_space=pltpu.VMEM)


def params(mib, semantics=None):
    return pltpu.CompilerParams(vmem_limit_bytes=mib * 1024 * 1024, dimension_semantics=semantics)


def front(here, routes, lengths, feats, ids, buckets, rel, proj, table, vectors, w_qkv, w_ao):
    rows = MICRO * SEQ
    shapes = [
        in_vmem((rows, D), BF16),
        in_vmem((rows, D), BF16),
        in_vmem((rows, 3 * D), BF16),
        in_vmem((MICRO * HEADS, SEQ, SEQ), BF16),
        in_vmem((rows, D), BF16),
        in_vmem((rows, D), F32),
        in_vmem((rows, D), BF16),
        in_vmem((16, D), F32),
        in_vmem((1, 2 * SEQ), jnp.int32),
    ]
    return pl.pallas_call(
        front_kernel,
        out_shape=shapes,
        in_specs=[smem()] * 3 + [vmem()] * 15 + [hbm()] * 2,
        out_specs=[vmem()] * 9,
        scratch_shapes=[
            pltpu.VMEM((D, 3 * D), BF16),
            pltpu.VMEM((D, D), BF16),
            pltpu.SemaphoreType.DMA((2,)),
            pltpu.VMEM((HEADS, SEQ, SEQ), BF16),
            pltpu.VMEM((MICRO, SEQ, SEQ), F32),
            pltpu.VMEM((16, 2 * SEQ), F32),
            pltpu.VMEM((ROWS, D), BF16),
        ],
        compiler_params=params(20),
        cost_estimate=pl.CostEstimate(flops=4_000_000_000, bytes_accessed=20_000_000, transcendentals=1_600_000),
        name="front",
    )(here, routes, lengths, *in_hbm(feats, ids, buckets, rel, proj, table, *vectors, w_qkv, w_ao))


def gelu_parts(before):
    cdf = 0.5 * (1.0 + lax.erf(before * 0.7071067811865476))
    pdf = jnp.exp(before * before * -0.5) * 0.3989422804014327
    return before * cdf, cdf + before * pdf


HALF = FF // 2


def ffn_kernel(
    other,
    here_ref, routes_ref, lengths_ref,
    h2_ref, vec_ref, cot_mine, cot_other, post_ref, win_hbm, wout_hbm,
    act_ref, gb_ref, enc_ref, gh_ref, ge_ref, cot_ref, dbin_ref,
    win_ref, wout_ref, sems,
):
    d = here_ref[0]
    who = 1 - d if other else d
    copies = []
    for n in range(HALF // 256):
        at = aligned(d * HALF + n * 256, 256)
        cols = slice(n * 256, (n + 1) * 256)
        copies.append((
            pltpu.make_async_copy(win_hbm.at[:, at], win_ref.at[:, cols], sems.at[0, n]),
            pltpu.make_async_copy(wout_hbm.at[at, :], wout_ref.at[cols, :], sems.at[1, n]),
        ))
        for copy in copies[-1]:
            copy.start()
    for m in range(MICRO):
        modality, _ = route_of(routes_ref, who, m, 0)
        first = lengths_ref[m, 0, who, 0]
        second = lengths_ref[m, 0, who, 1]
        post = jnp.where(modality == 0, post_ref[:, 0, :].astype(F32), post_ref[:, 1, :].astype(F32)).astype(BF16)
        for j in range(2):
            _, block = route_of(routes_ref, who, m, j)
            rows = slice((m * 2 + j) * ROWS, (m * 2 + j + 1) * ROWS)
            limit = jnp.where(modality == 0, first + second - j * ROWS, (first, second)[j])
            at_block = aligned(block * ROWS, ROWS)
            picked = jnp.where(
                modality == d,
                cot_mine[:, m, at_block].astype(F32),
                cot_other[:, m, at_block].astype(F32),
            )
            picked = jnp.where(iota(picked.shape, 1) < limit, picked, 0.0).astype(BF16)
            cot_ref[:, rows] = picked
            ge_ref[rows, :] = dot_tn(picked, post).astype(BF16)

    for n in range(HALF // 256):
        for copy in copies[n]:
            copy.wait()
        cols = slice(n * 256, (n + 1) * 256)
        bias = vec_ref[pl.ds(BFI + d * 2 + n // 3, 1), n % 3 * 256 : (n % 3 + 1) * 256]
        before = dot(h2_ref[...], win_ref[:, cols]) + bias
        grad = dot_nt(ge_ref[...], wout_ref[cols, :])
        value, slope = gelu_parts(before)
        act_ref[:, cols] = value.astype(BF16)
        low = (grad * slope).astype(BF16)
        gb_ref[:, cols] = low
        dbin_ref[0:1, cols] = jnp.sum(low.astype(F32), axis=0, keepdims=True)
    for n in range(D // 256):
        cols = slice(n * 256, (n + 1) * 256)
        enc_ref[:, cols] = dot(act_ref[...], wout_ref[:, cols])
        gh_ref[:, cols] = dot_nt(gb_ref[...], win_ref[cols, :])


def ffn(other, here, routes, lengths, h2, vecs, cot_mine, cot_other, post, w_in, w_out):
    rows = MICRO * SEQ
    return pl.pallas_call(
        functools.partial(ffn_kernel, other),
        out_shape=[
            in_vmem((rows, HALF), BF16),
            in_vmem((rows, HALF), BF16),
            in_vmem((rows, D), F32),
            in_vmem((rows, D), F32),
            in_vmem((rows, D), BF16),
            in_vmem((OUT, rows), BF16),
            in_vmem((8, HALF), F32),
        ],
        in_specs=[smem()] * 3 + [vmem()] * 5 + [hbm()] * 2,
        out_specs=[vmem()] * 7,
        scratch_shapes=[
            pltpu.VMEM((D, HALF), BF16), pltpu.VMEM((HALF, D), BF16), pltpu.SemaphoreType.DMA((2, HALF // 256)),
        ],
        compiler_params=params(16),
        cost_estimate=pl.CostEstimate(flops=5_000_000_000, bytes_accessed=20_000_000, transcendentals=1_600_000),
        name="ffn",
    )(here, routes, lengths, *resident(h2, vecs), *in_hbm(cot_mine), *resident(cot_other), *in_hbm(post, w_in, w_out))


def spread(links, here_ref, out, first, values, first_col):
    own = links.spot(here_ref[0], here_ref[1])
    groups = out.shape[0] // (16 * links.parts)
    width = values.shape[1]
    for i in range(values.shape[0] // 16):
        granule = first // 16 + i
        group, part = granule // links.parts, granule % links.parts
        rows = pl.ds(pl.multiple_of(((part ^ own) * groups + group) * 16, 16), 16)
        out[rows, first_col : first_col + width] = values[i * 16 : (i + 1) * 16, :]


def grad_rows_kernel(links, here_ref, left_mine, left_other, right_mine, right_other, keep_ref, send_ref, total):
    for i in range(left_mine.shape[1] // 256):
        cols = slice(i * 256, (i + 1) * 256)
        part = dot_tn(left_mine[:, cols], right_mine[...]) + dot_tn(left_other[:, cols], right_other[...])
        spread(links, here_ref, total, i * 256, part.astype(BF16), 0)
    half = keep_ref.shape[0]
    keep_ref[...] = total[:half, :]
    send_ref[...] = total[half:, :]


def grad_rows(links, left_mine, left_other, right_mine, right_other):
    width = right_mine.shape[1]
    height = links.padded(left_mine.shape[1])
    return pl.pallas_call(
        functools.partial(grad_rows_kernel, links),
        out_shape=[in_vmem((height // 2, width), BF16)] * 2,
        in_specs=[smem()] + [vmem()] * 4,
        out_specs=[vmem()] * 2,
        scratch_shapes=[pltpu.VMEM((height, width), BF16)],
        compiler_params=params(16),
        cost_estimate=pl.CostEstimate(flops=2_400_000_000, bytes_accessed=7_000_000, transcendentals=0),
        name="grad_rows",
    )(links.here, *resident(left_mine, left_other, right_mine, right_other))


def grad_mixed_kernel(links, here_ref, ctx_mine, ctx_other, gbr_mine, gbr_other, e_mine, e_other, keep_ref, send_ref, total):
    for i in range(D // 256):
        cols = slice(i * 256, (i + 1) * 256)
        part = dot_tn(ctx_mine[:, cols], gbr_mine[...]) + dot_tn(ctx_other[:, cols], gbr_other[...])
        spread(links, here_ref, total, i * 256, part.astype(BF16), 0)
        part = e_mine[cols, :].astype(F32) + e_other[cols, :].astype(F32)
        spread(links, here_ref, total, i * 256, part.astype(BF16), 384)
    half = keep_ref.shape[0]
    keep_ref[...] = total[:half, :]
    send_ref[...] = total[half:, :]


def grad_mixed(links, ctx_mine, ctx_other, gbr_mine, gbr_other, e_mine, e_other):
    height = links.padded(D)
    return pl.pallas_call(
        functools.partial(grad_mixed_kernel, links),
        out_shape=[in_vmem((height // 2, 768), BF16)] * 2,
        in_specs=[smem()] + [vmem()] * 6,
        out_specs=[vmem()] * 2,
        scratch_shapes=[pltpu.VMEM((height, 768), BF16)],
        compiler_params=params(12),
        cost_estimate=pl.CostEstimate(flops=600_000_000, bytes_accessed=5_000_000, transcendentals=0),
        name="grad_mixed",
    )(links.here, *resident(ctx_mine, ctx_other, gbr_mine, gbr_other, e_mine, e_other))


def column_sum(values):
    return jnp.sum(values, axis=0, keepdims=True)


def attend_back_kernel(
    here_ref, gh_ref, gh_other, mid_ref, ge_ref, vec_ref, qkv_ref, pt_ref, bucket_ref, wao_hbm,
    gm_ref, gbr_mine, gbr_other, gq_mine, gq_other, rel_ref, sums_ref,
    gctx, frow, gbr_ref, gqkv_ref, wao_ref, sem,
):
    d = here_ref[0]
    copy_ao = pltpu.make_async_copy(wao_hbm, wao_ref, sem)
    copy_ao.start()
    sums_ref[...] = jnp.zeros_like(sums_ref)
    frow[...] = jnp.zeros_like(frow)

    def second_norm(r, _):
        rows = aligned(r * ROWS, ROWS)
        normed, inverse = normalise(mid_ref[rows, :])
        grad = gh_ref[rows, :] + gh_other[rows, :]
        ge = ge_ref[rows, :].astype(F32)
        gm = ge + norm_back(grad, normed, inverse, vec_ref[G2 : G2 + 1, :])
        gm_ref[rows, :] = gm
        low = gm.astype(BF16)
        gbr_ref[rows, :] = low
        sums_ref[0:1, :] += column_sum(grad * normed)
        sums_ref[1:2, :] += column_sum(grad)
        sums_ref[2:3, :] += column_sum(low.astype(F32))
        sums_ref[3:4, :] += column_sum(ge)
        return 0

    lax.fori_loop(0, MICRO * SEQ // ROWS, second_norm, 0)
    copy_ao.wait()
    for n in range(3):
        cols = slice(n * 256, (n + 1) * 256)
        gctx[:, cols] = dot_nt(gbr_ref[...], wao_ref[cols, :]).astype(BF16)
    low, high = head_masks()

    def attention(pair, _):
        at_q = aligned(pair * 128, 128)
        at_k = aligned(D + pair * 128, 128)
        at_v = aligned(2 * D + pair * 128, 128)
        grads = [[jnp.zeros((SEQ, 128), F32)] * 3 for _ in range(MICRO)]
        for s, keep in enumerate((low, high)):
            both = None
            for m in range(MICRO):
                rows = slice(m * SEQ, (m + 1) * SEQ)
                q = qkv_ref[rows, at_q]
                k = qkv_ref[rows, at_k]
                v = qkv_ref[rows, at_v]
                gc = gctx[rows, at_q]
                weights = pt_ref[m * HEADS + 2 * pair + s]
                wide = weights.astype(F32)
                gp = dot_nt(v * keep, gc)
                inner = jnp.sum(gp * wide, axis=0, keepdims=True)
                gs = wide * (gp - inner)
                both = gs if both is None else both + gs
                scaled = (gs * HEAD_DIM ** (-0.5)).astype(BF16)
                gq, gk, gv = grads[m]
                grads[m] = [
                    gq + dot_tn(scaled, k * keep),
                    gk + dot(scaled, q * keep),
                    gv + dot(weights, gc * keep),
                ]
            acc = None
            for a in range(SEQ // 8):
                part = jnp.concatenate([both[8 * a : 8 * a + 8, :], jnp.zeros((8, SEQ), F32)], axis=1)
                part = pltpu.roll(part, 2 * SEQ - 8 * a, 1) if a else part
                acc = part if acc is None else acc + part
            for bit in (1, 2, 4):
                moved = pltpu.roll(acc, 2 * SEQ - bit, 1)
                acc = jnp.where((iota(acc.shape, 0) & bit) != 0, moved, acc)
            frow[pl.ds(2 * pair + s, 1), :] = jnp.sum(acc, axis=0, keepdims=True)
        for m in range(MICRO):
            rows = slice(m * SEQ, (m + 1) * SEQ)
            for at, grad in zip((at_q, at_k, at_v), grads[m]):
                gqkv_ref[rows, at] = grad.astype(BF16)
        return 0

    lax.fori_loop(0, HEADS // 2, attention, 0)
    hot = (iota((rel_ref.shape[1], 2 * SEQ), 0) == bucket_ref[...]).astype(F32).astype(BF16)
    rest = frow[...]
    rel = jnp.zeros(rel_ref.shape, F32)
    for _ in range(3):
        term = rest.astype(BF16)
        rest = rest - term.astype(F32)
        rel = rel + dot_nt(term, hot)
    rel_ref[...] = rel
    for mine, whole, width in ((gbr_mine, gbr_ref, 384), (gq_mine, gqkv_ref, 1152)):
        mine[...] = whole[:, pl.ds(pl.multiple_of(d * width, 128), width)]
    for other, whole, width in ((gbr_other, gbr_ref, 384), (gq_other, gqkv_ref, 1152)):
        other[...] = whole[:, pl.ds(pl.multiple_of((1 - d) * width, 128), width)]
    sums_ref[4:5, :] = column_sum(gqkv_ref[:, 0:D].astype(F32))
    sums_ref[5:6, :] = column_sum(gqkv_ref[:, 2 * D : 3 * D].astype(F32))


def attend_back(here, gh, gh_other, mid, ge, vecs, qkv, pt, bucket_row, w_ao, buckets):
    rows = MICRO * SEQ
    return pl.pallas_call(
        attend_back_kernel,
        out_shape=[
            in_vmem((rows, D), F32),
            in_vmem((rows, 384), BF16),
            in_vmem((rows, 384), BF16),
            in_vmem((rows, 1152), BF16),
            in_vmem((rows, 1152), BF16),
            in_vmem((16, buckets), F32),
            in_vmem((8, D), F32),
        ],
        in_specs=[smem()] + [vmem()] * 8 + [hbm()],
        out_specs=[vmem()] * 7,
        scratch_shapes=[
            pltpu.VMEM((rows, D), BF16), pltpu.VMEM((16, 2 * SEQ), F32),
            pltpu.VMEM((rows, D), BF16), pltpu.VMEM((rows, 3 * D), BF16),
            pltpu.VMEM((D, D), BF16), pltpu.SemaphoreType.DMA(()),
        ],
        compiler_params=params(20),
        cost_estimate=pl.CostEstimate(flops=5_000_000_000, bytes_accessed=16_000_000, transcendentals=0),
        name="attend_back",
    )(here, *resident(gh, gh_other, mid, ge, vecs, qkv, pt, bucket_row), *in_hbm(w_ao))


def input_back_kernel(
    here_ref, routes_ref,
    gq_mine, gq_other, x_ref, gm_ref, vec_ref, mid_ref, enc_mine, enc_other, cot_ref,
    rel_ref, sums_ref, dbin_mine, dbin_other, ids_ref, wqkv_hbm, feats_hbm,
    enc_ref, eg_ref, e_mine, e_other, small_ref,
    total, wqkv_ref, feats_ref, sems,
):
    d = here_ref[0]
    copy_qkv = pltpu.make_async_copy(wqkv_hbm, wqkv_ref, sems.at[0])
    copy_feats = pltpu.make_async_copy(feats_hbm, feats_ref, sems.at[1])
    copy_qkv.start()
    copy_feats.start()
    small_ref[...] = jnp.zeros_like(small_ref)
    at_mine = pl.ds(pl.multiple_of(d * 1152, 128), 1152)
    at_other = pl.ds(pl.multiple_of((1 - d) * 1152, 128), 1152)

    for r in range(MICRO * SEQ // ROWS):
        rows = slice(r * ROWS, (r + 1) * ROWS)
        enc = mid_ref[rows, :] + vec_ref[BFO : BFO + 1, :] + enc_mine[rows, :] + enc_other[rows, :]
        enc_ref[rows, :] = enc.astype(BF16)
    copy_qkv.wait()

    def first_norm(r, _):
        rows = aligned(r * ROWS, ROWS)
        normed, inverse = normalise(x_ref[rows, :].astype(F32))
        grad = dot_nt(gq_mine[rows, :], wqkv_ref[:, at_mine]) + dot_nt(gq_other[rows, :], wqkv_ref[:, at_other])
        eg = gm_ref[rows, :] + norm_back(grad, normed, inverse, vec_ref[G1 : G1 + 1, :])
        eg_ref[rows, :] = eg.astype(BF16)
        small_ref[G1 : G1 + 1, :] += column_sum(grad * normed)
        small_ref[S1 : S1 + 1, :] += column_sum(grad)
        return 0

    lax.fori_loop(0, MICRO * SEQ // ROWS, first_norm, 0)
    copy_feats.wait()
    proj = total.at[0:512, :]
    rest = total.at[512:768, :]
    total[...] = jnp.zeros_like(total)
    for m in range(MICRO):
        modality, _ = route_of(routes_ref, d, m, 0)
        rows = slice(m * SEQ, (m + 1) * SEQ)
        blocks = [route_of(routes_ref, d, m, j)[1] for j in range(2)]
        post = dot(cot_ref[:, rows], enc_ref[rows, :])

        @pl.when(modality == 0)
        def _(m=m, rows=rows, blocks=blocks, post=post):
            for j, block in enumerate(blocks):
                feats = feats_ref[m, aligned(block * ROWS, ROWS), :]
                proj[...] += dot_tn(feats, eg_ref[m * SEQ + j * ROWS : m * SEQ + (j + 1) * ROWS, :])
            small_ref[SB : SB + 1, :] += column_sum(eg_ref[rows, :].astype(F32))
            rest[OUT : 2 * OUT, :] += post

        @pl.when(modality != 0)
        def _(m=m, rows=rows, blocks=blocks, post=post):
            table = jnp.zeros((ROWS, D), F32)
            for j, block in enumerate(blocks):
                hot = onehot_vocab(ids_ref, m, block)
                table = table + dot(hot, eg_ref[m * SEQ + j * ROWS : m * SEQ + (j + 1) * ROWS, :])
            rest[0:OUT, :] += table[0:OUT, :]
            rest[2 * OUT : 3 * OUT, :] += post

    for out, half in ((e_mine, d), (e_other, 1 - d)):
        out[...] = total[:, pl.ds(pl.multiple_of(half * 384, 128), 384)].astype(BF16)
    for at, row in ((G2, 0), (S2, 1), (BAO, 2), (BFO, 3), (BQ, 4), (BV, 5)):
        small_ref[at : at + 1, :] = sums_ref[row : row + 1, :]
    for i in range(2):
        cols = slice(i * D, (i + 1) * D)
        small_ref[pl.ds(BFI + d * 2 + i, 1), :] = dbin_mine[0:1, cols] + dbin_other[0:1, cols]
    small_ref[REL_ROW : REL_ROW + 16, 0 : rel_ref.shape[1]] = rel_ref[...]


def input_back(
    here, routes, gq_mine, gq_other, x, gm, vecs, mid, enc_mine, enc_other, cot, rel, sums, dbin_mine, dbin_other,
    ids, w_qkv, feats,
):
    rows = MICRO * SEQ
    return pl.pallas_call(
        input_back_kernel,
        out_shape=[
            jax.ShapeDtypeStruct((rows, D), BF16),
            jax.ShapeDtypeStruct((rows, D), BF16),
            in_vmem((D, 384), BF16),
            in_vmem((D, 384), BF16),
            in_vmem((SMALL_ROWS, D), F32),
        ],
        in_specs=[smem()] * 2 + [vmem()] * 14 + [hbm()] * 2,
        out_specs=[vmem()] * 5,
        scratch_shapes=[
            pltpu.VMEM((D, D), F32), pltpu.VMEM((D, 3 * D), BF16), pltpu.VMEM(feats.shape, BF16),
            pltpu.SemaphoreType.DMA((2,)),
        ],
        compiler_params=params(20),
        cost_estimate=pl.CostEstimate(flops=2_500_000_000, bytes_accessed=20_000_000, transcendentals=0),
        name="input_back",
    )(
        here, routes,
        *resident(gq_mine, gq_other, x, gm, vecs, mid, enc_mine, enc_other, cot, rel, sums, dbin_mine, dbin_other),
        *in_hbm(ids, w_qkv, feats),
    )


class Links:
    def __init__(self, mesh):
        self.nb = mesh.shape["batch"]
        self.nz = self.nb // 4
        self.line = self.nz.bit_length() - 1
        self.parts = 4 * self.nz
        self.c = lax.axis_index("mod")
        self.batch = lax.axis_index("batch")
        self.order = ["p", "q"] + list(range(self.line))
        self.here = jnp.stack([self.c, self.batch]).astype(jnp.int32)

    def bit(self, kind, c, batch):
        low, high = batch & 1, (batch >> 1) & 1
        if kind == "p":
            return jnp.where(c == 0, low, high)
        if kind == "q":
            return jnp.where(c == 0, high, low)
        z = batch >> 2
        return ((z >> kind) ^ (z >> (kind + 1))) & 1

    def spot(self, c, batch):
        at = 0
        for kind in self.order:
            at = at * 2 + self.bit(kind, c, batch)
        return at

    def padded(self, rows):
        return -(-rows // (16 * self.parts)) * 16 * self.parts

    def swap(self, kind, v):
        def partner(c, b):
            if kind == "m":
                return 1 - c, b
            if kind in ("p", "q"):
                return c, b ^ (1 if (kind == "p") == (c == 0) else 2)
            return c, b ^ (4 * (2 ** (kind + 1) - 1))

        pairs = []
        for c in range(2):
            for b in range(self.nb):
                c2, b2 = partner(c, b)
                pairs.append((c * self.nb + b, c2 * self.nb + b2))
        return lax.ppermute(v, AXES, pairs)


class Line:
    def __init__(self, token):
        self.token = token

    def after(self, *values):
        held = lax.optimization_barrier((values, self.token))[0]
        return held if len(held) > 1 else held[0]

    def done(self, value):
        self.token = value


class Chunk:
    def __init__(self, links, line, keep, send):
        self.links, self.line, self.order = links, line, links.order
        self.keep = keep
        self.level = 0
        self.got = links.swap(self.order[0], send)
        line.done(send)

    def step(self):
        links, line, order = self.links, self.line, self.order
        got = line.after(self.got)
        self.level += 1
        if self.level < len(order):
            half = got.shape[0] // 2
            send = (self.keep[half:].astype(F32) + got[half:].astype(F32)).astype(BF16)
            self.keep = (self.keep[:half].astype(F32) + got[:half].astype(F32)).astype(BF16)
            self.got = links.swap(order[self.level], send)
            line.done(send)
            return
        if self.level == len(order):
            self.own = (self.keep.astype(F32) + got.astype(F32)).astype(BF16)
        else:
            self.own = jnp.concatenate([self.own, got], axis=0)
        at = 2 * len(order) - 1 - self.level
        self.got = links.swap(order[at], self.own)
        line.done(self.own)
        if at == 0:
            self.other = links.swap("m", self.own)

    def last(self):
        while self.level < 2 * len(self.order) - 1:
            self.step()
        got = self.line.after(self.got)
        self.far = got
        self.far_other = self.links.swap("m", got)
        self.line.done(got)

    def place(self, outs):
        mine, far = self.own, self.far
        other, far_other = self.line.after(self.other, self.far_other)
        results = place(self.links, (mine, far, other, far_other), outs)
        self.line.done(results[0])
        return results


def place_kernel(links, outs, here_ref, *refs):
    ins, out_refs = refs[:4], refs[4:]
    step = pl.program_id(0)
    groups = 2 * ins[0].shape[0] // (16 * links.parts)
    for core in range(2):
        own = links.spot(jnp.where(core == 0, here_ref[0], 1 - here_ref[0]), here_ref[1])
        for group in range(groups):

            @pl.when(step == core * groups + group)
            def _(core=core, group=group, own=own):
                for out, (_, col, width, first, last) in zip(out_refs, outs):
                    if not first <= group < last:
                        continue
                    for part in range(links.parts):
                        ref = ins[core * 2 + part // (links.parts // 2)]
                        at = (part % (links.parts // 2) * groups + group) * 16
                        rows = pl.ds(pl.multiple_of((part ^ own) * 16, 16), 16)
                        out[rows, :] = ref[at : at + 16, col : col + width].astype(F32)


def place(links, gathered, outs):
    group = 16 * links.parts
    groups = 2 * gathered[0].shape[0] // group

    def block_of(rows_first, first, last):
        def index(s, here):
            core = jnp.where(s < groups, here[0], 1 - here[0])
            at = jnp.clip(s % groups, first, last - 1) - first
            return (core * (last - first) + at, 0) if rows_first else (at, core)

        return index

    shapes, specs = [], []
    for rows_first, _, width, first, last in outs:
        tall = (last - first) * group
        shapes.append((2 * tall, width) if rows_first else (tall, 2 * width))
        specs.append(pl.BlockSpec((group, width), block_of(rows_first, first, last)))
    return pl.pallas_call(
        functools.partial(place_kernel, links, outs),
        out_shape=[jax.ShapeDtypeStruct(s, F32) for s in shapes],
        grid_spec=pltpu.PrefetchScalarGridSpec(
            num_scalar_prefetch=1,
            grid=(2 * groups,),
            in_specs=[vmem()] * 4,
            out_specs=specs,
        ),
        compiler_params=params(16, ("arbitrary",)),
        cost_estimate=pl.CostEstimate(flops=1_000_000, bytes_accessed=24 * gathered[0].size, transcendentals=0),
        name="place",
    )(links.here, *resident(*gathered))


class Small:
    def __init__(self, links, line, kinds, value):
        self.links, self.line, self.kinds = links, line, list(kinds)
        self.value = value
        self.got = links.swap(self.kinds.pop(0), value)

    def step(self):
        got = self.line.after(self.got)
        self.value = self.value + got
        self.got = self.links.swap(self.kinds.pop(0), self.value) if self.kinds else None
        self.line.done(self.value)


ORDER = (
    "A C B S A C D B A S C D B A C S D B A C D S B Al C D S Bl C D Aw Cl D Bw Dl Cw Dw"
)


def out_rows(v, tall):
    return v if tall == HALF else jnp.concatenate([v[:HALF], v[tall : tall + HALF]], axis=0)


def on_device(
    mesh,
    speech_feats, text_ids, routes, lengths, buckets, post_cot,
    ln1_gain, ln1_bias, w_qkv, bias_qv, rel_table, w_attn_out, bias_attn_out,
    ln2_gain, ln2_bias, w_ffn_in, bias_ffn_in, w_ffn_out, bias_ffn_out,
    speech_proj, speech_bias, text_table, post_weight,
):
    links = Links(mesh)
    here = links.here
    cot_mine = jnp.transpose(post_cot[0], (2, 0, 1))
    cot_other = links.swap("m", cot_mine)
    post = jnp.transpose(post_weight, (2, 0, 1))
    x, h1, qkv, pt, ctx, mid, h2, vecs, bucket_row = front(
        here, routes, lengths, speech_feats, text_ids, buckets, jnp.transpose(rel_table), speech_proj, text_table,
        (ln1_gain, ln1_bias, bias_qv, bias_attn_out, ln2_gain, ln2_bias, bias_ffn_out, speech_bias, bias_ffn_in),
        w_qkv, w_attn_out,
    )
    h2_other = links.swap("m", h2)
    h1_other = links.swap("m", h1)
    ctx_other = links.swap("m", ctx)
    line = Line(h2)

    def ffn_rows(other, h2):
        return ffn(other, here, routes, lengths, h2, vecs, cot_mine, cot_other, post, w_ffn_in, w_ffn_out)

    act, gb, enc, gh, ge, cot, dbin = ffn_rows(False, h2)
    line.done(enc)
    act_o, gb_o, enc_o, gh_o, ge_o, _, dbin_o = ffn_rows(True, line.after(h2_other))
    line.done(enc_o)
    gh_got = links.swap("m", gh_o)
    enc_got = links.swap("m", enc_o)
    chunk = {}
    chunk["A"] = Chunk(links, line, *grad_rows(links, line.after(act), act_o, ge, ge_o))
    chunk["B"] = Chunk(links, line, *grad_rows(links, line.after(h2), h2_other, gb, gb_o))
    gm, gbr, gbr_send, gq, gq_send, drel, sums = attend_back(
        here, line.after(gh), gh_got, mid, ge, vecs, qkv, pt, bucket_row, w_attn_out, rel_table.shape[0]
    )
    line.done(gm)
    gq_got = links.swap("m", gq_send)
    gbr_got = links.swap("m", gbr_send)
    chunk["A"].step()
    chunk["B"].step()
    encoded, eg, e_mine, e_send, small = input_back(
        here, routes, gq, gq_send, x, line.after(gm), vecs, mid, enc, enc_got, cot, drel, sums, dbin, dbin_o,
        text_ids, w_qkv, speech_feats,
    )
    line.done(eg)
    e_got = links.swap("m", e_send)
    chunk["A"].step()
    chunk["C"] = Chunk(links, line, *grad_rows(links, line.after(h1), h1_other, gq, gq_got))
    chunk["B"].step()
    chunk["D"] = Chunk(links, line, *grad_mixed(links, line.after(ctx), ctx_other, gbr, gbr_got, e_mine, e_got))
    chunk["S"] = Small(links, line, ["m"] + links.order, small)
    groups = links.padded(D) // (16 * links.parts)
    split = 512 // (16 * links.parts)
    outs = {
        "A": ((True, 0, D, 0, links.padded(HALF) // (16 * links.parts)),),
        "B": ((False, 0, HALF, 0, groups),),
        "C": ((False, 0, 1152, 0, groups),),
        "D": (
            (False, 0, 384, 0, groups),
            (False, 384, 384, 0, max(split, 1)),
            (False, 384, 384, min(split, groups - 1), groups),
        ),
    }
    placed = {}
    for name in ORDER.split():
        if name[-1] == "l":
            chunk[name[0]].last()
        elif name[-1] == "w":
            placed[name[0]] = chunk[name[0]].place(outs[name[0]])
        else:
            chunk[name].step()
    (g_out,), (g_in,), (g_qkv,), (g_ao, g_proj, g_rest) = (placed[k] for k in "ABCD")
    while chunk["S"].got is not None:
        chunk["S"].step()
    small = chunk["S"].value
    rows = text_ids.shape[0]
    g_rest = g_rest[512 - 16 * links.parts * min(split, groups - 1) :]
    g_post = jnp.transpose(g_rest[OUT : 3 * OUT].reshape(2, OUT, D), (0, 2, 1))
    return (
        encoded.reshape(rows, SEQ, D),
        eg.reshape(rows, SEQ, D),
        small[G1],
        small[S1],
        g_qkv[:D],
        small[BQ : BQ + 2],
        small[REL_ROW : REL_ROW + HEADS, 0 : rel_table.shape[0]].T,
        g_ao[:D],
        small[BAO],
        small[G2],
        small[S2],
        g_in[:D],
        small[BFI : BFI + 4].reshape(FF),
        out_rows(g_out, links.padded(HALF)),
        small[BFO],
        g_proj[:512],
        small[SB],
        g_rest[:OUT],
        g_post,
    )


def solution(mesh):
    batch = P(None, "batch", None)
    rows = P(None, AXES, None)
    return jax.shard_map(
        functools.partial(on_device, mesh),
        mesh=mesh,
        in_specs=(
            batch, P(None, "batch"), P(None, "batch", None, None), P(None, "batch", None, None), P(),
            P("mod", None, "batch", None),
        ) + (P(),) * 17,
        out_specs=(rows, rows) + (P(),) * 17,
        check_vma=False,
    )
```

time: 344 us -> 236 us (0.69)
  waiting for transfers between devices: 119 us -> 66.5 us
  local copies, waits for them, and re-layouts: 34.9 us -> 5.69 us
  Pallas kernels: 110 us -> 94.8 us
  starting transfers between devices: 70.3 us -> 61.4 us
  other arithmetic: 8.54 us -> 2.4 us
    ppermute x55 -> x54, waiting for transfers between devices: 119 us -> 66.5 us  [swap(): return lax.ppermute(v, AXES, pairs)]
    pallas_call x7 -> x12, Pallas kernels: 88.8 us -> 77.7 us  [the longest x4 22.3 us: place(): pl.pallas_call(functools.partial(place_kernel, links, outs), out_shape=[j...]
    unnamed x68 -> x11, local copies, waits for them, and re-layouts: 12 us -> 2.41 us
    ppermute x55 -> x54, starting transfers between devices: 70.3 us -> 61.4 us  [swap(): return lax.ppermute(v, AXES, pairs)]
    slice x6 -> x2, local copies, waits for them, and re-layouts: 8.03 us -> 0.76 us  [the longest x1 0.72 us: on_device(): g_rest[:OUT]]
    dynamic_slice x6 -> x0, local copies, waits for them, and re-layouts: 4.34 us -> none  [pick(): return lax.dynamic_index_in_dim(v, i, 0, keepdims=False)]
    convert_element_type x12 -> x16, other arithmetic: 6.01 us -> 1.76 us  [the longest x7 1.3 us: step(): (self.keep[:half].astype(F32) + got[:half].astype(F32)).astype(BF16)]
    pallas_call x1, Pallas kernels: 20.8 us -> 17.1 us  [front(): pl.pallas_call(front_kernel, out_shape=shapes, in_specs=[smem()] * 3 + [v...]
  transfers between devices with their start and end apart: 55 -> 54, of which waited for: 19 -> 21; matrix products, arithmetic and copies ran while one was open for 10% -> 2% of each run, Pallas kernels for 25% -> 27%
where the time goes in v1:
time: 236 us; the launch traced here: 232 us
  Pallas kernels  94.8 us (40%)
  waiting for transfers between devices  66.5 us (28%)
  starting transfers between devices  61.4 us (26%)
  local copies, waits for them, and re-layouts  5.69 us (2%)
  other arithmetic  2.4 us (1%)
    ppermute x54, waiting for transfers between devices, swap(): return lax.ppermute(v, AXES, pairs)  66.5 us
    ppermute x54, starting transfers between devices, swap(): return lax.ppermute(v, AXES, pairs)  61.4 us
    pallas_call x4, Pallas kernels, place(): pl.pallas_call(functools.partial(place_kernel, links, outs), out_shape=[j...  22.3 us
    pallas_call x2, Pallas kernels, ffn(): pl.pallas_call(functools.partial(ffn_kernel, other), out_shape=[in_vmem((...  20.6 us
    pallas_call x1, Pallas kernels, front(): pl.pallas_call(front_kernel, out_shape=shapes, in_specs=[smem()] * 3 + [v...  17.1 us
    pallas_call x1, Pallas kernels, attend_back(): pl.pallas_call(attend_back_kernel, out_shape=[in_vmem((rows, D), F32), in...  12.3 us
    pallas_call x1, Pallas kernels, input_back(): pl.pallas_call(input_back_kernel, out_shape=[jax.ShapeDtypeStruct((rows,...  11 us
    pallas_call x3, Pallas kernels, grad_rows(): pl.pallas_call(functools.partial(grad_rows_kernel, links), out_shape=[in_...  9.72 us
  transfers between devices with their start and end apart: 54, of which 21 were waited for; matrix products, arithmetic and copies ran while one was open for 2% of the time, Pallas kernels for 27%

profile of v1, /device:TPU:0, one launch (start us, length us, event | category | flops | bytes accessed | tf_op | source)
XLA Modules:
  0.0 232.3 jit_solution(13619930647337495603)
XLA Ops:
  2.1 17.1 %front.1 = (bf16[512,768]{1,0:T(8,128)(2,1)S(1)}, bf16[512,768]{1,0:T(8,128)(2,1)S(1)}, bf16[512,2304]{1,0:T(8,128)(2,1)S(1)}, bf16[24,256,256]{2,1,0:T(8,128)(2...) custom-call(s32[2]{0:T(128)S(1)} %pad_add_fusion.here_ref, ...), custom_call_target="tpu_custom_call" | custom-call | flops 4000000000 | bytes 20000000 | tf_op jit(solution)/shard_map/front/pallas_call | solution.py:241
  19.8 2.1 collective-permute-done.cot_other
  21.9 9.9 %ffn.2 = (bf16[512,1536]{1,0:T(8,128)(2,1)S(1)}, bf16[512,1536]{1,0:T(8,128)(2,1)S(1)}, f32[512,768]{1,0:T(8,128)S(1)}, f32[512,768]{1,0:T(8,128)S(1)}, bf16[512...) custom-call(s32[2]{0:T(128)S(1)} %pad_add_fusion.here_ref, s32[2,1,2,2]{3,2,1,0:T(2,128)S(1)} %copy-done, ...), custom_call_target="tpu_custom_call" | custom-call | flops 5000000000 | bytes 20000000 | tf_op jit(solution)/shard_map/ffn/pallas_call | solution.py:328
  31.8 10.7 %ffn.3 = (bf16[512,1536]{1,0:T(8,128)(2,1)S(1)}, bf16[512,1536]{1,0:T(8,128)(2,1)S(1)}, f32[512,768]{1,0:T(8,128)S(1)}, f32[512,768]{1,0:T(8,128)S(1)}, bf16[512...) custom-call(s32[2]{0:T(128)S(1)} %pad_add_fusion.here_ref, s32[2,1,2,2]{3,2,1,0:T(2,128)S(1)} %copy-done.1, ...), custom_call_target="tpu_custom_call" | custom-call | flops 5000000000 | bytes 20000000 | tf_op jit(solution)/shard_map/ffn/pallas_call | solution.py:328
  42.9 3.4 %grad_rows.3 = (bf16[768,768]{1,0:T(8,128)(2,1)S(1)}, bf16[768,768]{1,0:T(8,128)(2,1)S(1)}) custom-call(s32[2]{0:T(128)S(1)} %pad_add_fusion.here_ref, bf16[512,1536]{1,0:T(8,128)(2,1)S(1)} %get-tuple-element.123.left_mine, bf16[512,1536]{1,0:T(8,128)(2,1)S(1)} %get-tuple-element.124.left_other, bf16[512,768]{1,0:T(8,128)(2,1)S(1)} %get-tuple-element.125.right_mine.ge_ref, ...), custom_call_target="tpu_custom_call" | custom-call | flops 2400000000 | bytes 7000000 | tf_op jit(solution)/shard_map/grad_rows/pallas_call | solution.py:374
  46.3 2.8 %collective-permute-start.4 = (bf16[768,768]{1,0:T(8,128)(2,1)S(1)}, bf16[768,768]{1,0:T(8,128)(2,1)S(1)}, u32[]{:S(2)}, u32[]{:S(2)}) collective-permute-start(bf16[768,768]{1,0:T(8,128)(2,1)S(1)} %get-tuple-element.127), channel_id=1, source_target_pairs={{0,1},{1,0},{2,3},{3,2},{4,5},{5,4},{6,7},{7,6},{8,9},{9,8},{10,11... | collective-permute-start | bytes 3538952 | tf_op jit(solution)/shard_map/ppermute | solution.py:675
  49.1 3.4 %grad_rows.4 = (bf16[384,1536]{1,0:T(8,128)(2,1)S(1)}, bf16[384,1536]{1,0:T(8,128)(2,1)S(1)}) custom-call(s32[2]{0:T(128)S(1)} %pad_add_fusion.here_ref, bf16[512,768]{1,0:T(8,128)(2,1)S(1)} %get-tuple-element.128.h2_ref.left_mine, bf16[512,768]{1,0:T(8,128)(2,1)S(1)} %collective-permute-done.1.h2_ref.left_other, ...), custom_call_target="tpu_custom_call" | custom-call | flops 2400000000 | bytes 7000000 | tf_op jit(solution)/shard_map/grad_rows/pallas_call | solution.py:374
  53.2 12.3 %attend_back.1 = (f32[512,768]{1,0:T(8,128)S(1)}, bf16[512,384]{1,0:T(8,128)(2,1)S(1)}, bf16[512,384]{1,0:T(8,128)(2,1)S(1)}, bf16[512,1152]{1,0:T(8,128)(2,1)S(...) custom-call(s32[2]{0:T(128)S(1)} %pad_add_fusion.here_ref, ...), custom_call_target="tpu_custom_call" | custom-call | flops 5000000000 | bytes 16000000 | tf_op jit(solution)/shard_map/attend_back/pallas_call | solution.py:509
  66.4 9.6 %collective-permute-done.3 = bf16[384,1536]{1,0:T(8,128)(2,1)S(1)} collective-permute-done((bf16[384,1536]{1,0:T(8,128)(2,1)S(1)}, bf16[384,1536]{1,0:T(8,128)(2,1)S(1)}, u32[]{:S(2)}, u32[]{:S(2)}) %collective-permute-start.3) | collective-permute-done | bytes 1179680 | tf_op jit(solution)/shard_map/ppermute | solution.py:675
  76.0 2.0 collective-permute-start.8
  78.4 11.0 %input_back.1 = (bf16[512,768]{1,0:T(8,128)(2,1)}, bf16[512,768]{1,0:T(8,128)(2,1)}, bf16[768,384]{1,0:T(8,128)(2,1)S(1)}, bf16[768,384]{1,0:T(8,128)(2,1)S(1)}, f32[32,768]{1,0:T(8,128)S(1)}) custom-call(s32[2]{0:T(128)S(1)} %pad_add_fusion.here_ref, s32[2,1,2,2]{3,2,1,0:T(2,128)S(1)} %copy-done.1, ...), custom_call_target="tpu_custom_call" | custom-call | flops 2500000000 | bytes 20000000 | tf_op jit(solution)/shard_map/input_back/pallas_call | solution.py:608
  89.5 3.0 %grad_rows.5 = (bf16[384,1152]{1,0:T(8,128)(2,1)S(1)}, bf16[384,1152]{1,0:T(8,128)(2,1)S(1)}) custom-call(s32[2]{0:T(128)S(1)} %pad_add_fusion.here_ref, bf16[512,768]{1,0:T(8,128)(2,1)S(1)} %get-tuple-element.157.left_mine, bf16[512,768]{1,0:T(8,128)(2,1)S(1)} %collective-permute-done.9.left_other, ...), custom_call_target="tpu_custom_call" | custom-call | flops 2400000000 | bytes 7000000 | tf_op jit(solution)/shard_map/grad_rows/pallas_call | solution.py:374
  92.5 2.9 %collective-permute-start.12 = (bf16[384,1152]{1,0:T(8,128)(2,1)S(1)}, bf16[384,1152]{1,0:T(8,128)(2,1)S(1)}, u32[]{:S(2)}, u32[]{:S(2)}) collective-permute-start(bf16[384,1152]{1,0:T(8,128)(2,1)S(1)} %get-tuple-element.158), channel_id=1, source_target_pairs={{0,1},{1,0},{2,3},{3,2},{4,5},{5,4},{6,7},{7,6},{8,9},{9,8},{10,11... | collective-permute-start | bytes 2654216 | tf_op jit(solution)/shard_map/ppermute | solution.py:675
  98.6 1.8 grad_mixed.1
  100.4 1.5 collective-permute-start.21
  102.0 3.8 %collective-permute-done.13 = bf16[192,768]{1,0:T(8,128)(2,1)S(1)} collective-permute-done((bf16[192,768]{1,0:T(8,128)(2,1)S(1)}, bf16[192,768]{1,0:T(8,128)(2,1)S(1)}, u32[]{:S(2)}, u32[]{:S(2)}) %collective-permute-start.13) | collective-permute-done | bytes 294944 | tf_op jit(solution)/shard_map/ppermute | solution.py:675
  105.8 3.2 %collective-permute-start.18 = (bf16[96,768]{1,0:T(8,128)(2,1)S(1)}, bf16[96,768]{1,0:T(8,128)(2,1)S(1)}, u32[]{:S(2)}, u32[]{:S(2)}) collective-permute-start(bf16[96,768]{1,0:T(8,128)(2,1)S(1)} %add_convert_fusion.21), channel_id=1, source_target_pairs={{0,12},{1,13},{2,14},{3,15},{4,8},{5,9},{6,10},{7,11},{8,4},{9,5},... | collective-permute-start | bytes 442376 | tf_op jit(solution)/shard_map/ppermute | solution.py:675
  109.3 2.0 collective-permute-start.22
  111.3 6.2 %collective-permute-start.20 = (bf16[48,1536]{1,0:T(8,128)(2,1)S(1)}, bf16[48,1536]{1,0:T(8,128)(2,1)S(1)}, u32[]{:S(2)}, u32[]{:S(2)}) collective-permute-start(bf16[48,1536]{1,0:T(8,128)(2,1)S(1)} %add_convert_fusion.20), channel_id=1, source_target_pairs={{0,12},{1,13},{2,14},{3,15},{4,8},{5,9},{6,10},{7,11},{8,4},{9,5},... | collective-permute-start | bytes 442376 | tf_op jit(solution)/shard_map/ppermute | solution.py:675
  119.0 2.0 collective-permute-start.28
  121.4 3.7 %collective-permute-start.27 = (bf16[48,1536]{1,0:T(8,128)(2,1)S(1)}, bf16[48,1536]{1,0:T(8,128)(2,1)S(1)}, u32[]{:S(2)}, u32[]{:S(2)}) collective-permute-start(bf16[48,1536]{1,0:T(8,128)(2,1)S(1)} %add_convert_fusion.16), channel_id=1, source_target_pairs={{0,12},{1,13},{2,14},{3,15},{4,8},{5,9},{6,10},{7,11},{8,4},{9,5},... | collective-permute-start | bytes 442376 | tf_op jit(solution)/shard_map/ppermute | solution.py:675
  125.1 1.4 collective-permute-done.19
  126.5 6.3 %collective-permute-start.26 = (bf16[192,768]{1,0:T(8,128)(2,1)S(1)}, bf16[192,768]{1,0:T(8,128)(2,1)S(1)}, u32[]{:S(2)}, u32[]{:S(2)}) collective-permute-start(bf16[192,768]{1,0:T(8,128)(2,1)S(1)} %pad_maximum_fusion.7), channel_id=1, source_target_pairs={{0,4},{1,5},{2,6},{3,7},{4,0},{5,1},{6,2},{7,3},{8,12},{9,13},{10,... | collective-permute-start | bytes 884744 | tf_op jit(solution)/shard_map/ppermute | solution.py:675
  133.0 2.4 %collective-permute-start.25 = (bf16[48,1152]{1,0:T(8,128)(2,1)S(1)}, bf16[48,1152]{1,0:T(8,128)(2,1)S(1)}, u32[]{:S(2)}, u32[]{:S(2)}) collective-permute-start(bf16[48,1152]{1,0:T(8,128)(2,1)S(1)} %add_convert_fusion.23), channel_id=1, source_target_pairs={{0,12},{1,13},{2,14},{3,15},{4,8},{5,9},{6,10},{7,11},{8,4},{9,5},... | collective-permute-start | bytes 331784 | tf_op jit(solution)/shard_map/ppermute | solution.py:675
  135.6 2.1 collective-permute-start.34
  137.7 4.3 %collective-permute-done.26 = bf16[192,768]{1,0:T(8,128)(2,1)S(1)} collective-permute-done((bf16[192,768]{1,0:T(8,128)(2,1)S(1)}, bf16[192,768]{1,0:T(8,128)(2,1)S(1)}, u32[]{:S(2)}, u32[]{:S(2)}) %collective-permute-start.26) | collective-permute-done | bytes 294944 | tf_op jit(solution)/shard_map/ppermute | solution.py:675
  142.1 3.4 %collective-permute-done.25 = bf16[48,1152]{1,0:T(8,128)(2,1)S(1)} collective-permute-done((bf16[48,1152]{1,0:T(8,128)(2,1)S(1)}, bf16[48,1152]{1,0:T(8,128)(2,1)S(1)}, u32[]{:S(2)}, u32[]{:S(2)}) %collective-permute-start.25) | collective-permute-done | bytes 110624 | tf_op jit(solution)/shard_map/ppermute | solution.py:675
  145.6 1.5 collective-permute-start.32
  147.2 2.4 %collective-permute-start.31 = (bf16[48,768]{1,0:T(8,128)(2,1)S(1)}, bf16[48,768]{1,0:T(8,128)(2,1)S(1)}, u32[]{:S(2)}, u32[]{:S(2)}) collective-permute-start(bf16[48,768]{1,0:T(8,128)(2,1)S(1)} %add_convert_fusion.26), channel_id=1, source_target_pairs={{0,12},{1,13},{2,14},{3,15},{4,8},{5,9},{6,10},{7,11},{8,4},{9,5},... | collective-permute-start | bytes 221192 | tf_op jit(solution)/shard_map/ppermute | solution.py:675
  149.7 3.4 %collective-permute-done.34 = bf16[96,1536]{1,0:T(8,128)(2,1)S(1)} collective-permute-done((bf16[96,1536]{1,0:T(8,128)(2,1)S(1)}, bf16[96,1536]{1,0:T(8,128)(2,1)S(1)}, u32[]{:S(2)}, u32[]{:S(2)}) %collective-permute-start.34) | collective-permute-done | bytes 294944 | tf_op jit(solution)/shard_map/ppermute | solution.py:675
  153.7 2.1 collective-permute-start.38
  156.6 12.9 %collective-permute-done.39 = bf16[192,1536]{1,0:T(8,128)(2,1)S(1)} collective-permute-done((bf16[192,1536]{1,0:T(8,128)(2,1)S(1)}, bf16[192,1536]{1,0:T(8,128)(2,1)S(1)}, u32[]{:S(2)}, u32[]{:S(2)}) %collective-permute-start.39) | collective-permute-done | bytes 589856 | tf_op jit(solution)/shard_map/ppermute | solution.py:675
  170.0 1.2 collective-permute-start.37
  171.3 1.3 collective-permute-done.38.refs_1_
  172.5 3.4 %collective-permute-done.37 = bf16[96,1152]{1,0:T(8,128)(2,1)S(1)} collective-permute-done((bf16[96,1152]{1,0:T(8,128)(2,1)S(1)}, bf16[96,1152]{1,0:T(8,128)(2,1)S(1)}, u32[]{:S(2)}, u32[]{:S(2)}) %collective-permute-start.37) | collective-permute-done | bytes 221216 | tf_op jit(solution)/shard_map/ppermute | solution.py:675
  176.0 2.1 collective-permute-start.40
  178.1 1.3 collective-permute-start.36
  179.4 2.5 %collective-permute-start.35 = (f32[32,768]{1,0:T(8,128)S(1)}, f32[32,768]{1,0:T(8,128)S(1)}, u32[]{:S(2)}, u32[]{:S(2)}) collective-permute-start(f32[32,768]{1,0:T(8,128)S(1)} %add.130), channel_id=1, source_target_pairs={{0,12},{1,13},{2,14},{3,15},{4,8},{5,9},{6,10},{7,11},{8,4},{9,5},... | collective-permute-start | bytes 294920 | tf_op jit(solution)/shard_map/ppermute | solution.py:675
  181.9 3.1 %collective-permute-done.36 = bf16[48,768]{1,0:T(8,128)(2,1)S(1)} collective-permute-done((bf16[48,768]{1,0:T(8,128)(2,1)S(1)}, bf16[48,768]{1,0:T(8,128)(2,1)S(1)}, u32[]{:S(2)}, u32[]{:S(2)}) %collective-permute-start.36) | collective-permute-done | bytes 73760 | tf_op jit(solution)/shard_map/ppermute | solution.py:675
  185.1 1.7 collective-permute-done.35
  186.8 3.7 %collective-permute-done.41.refs_1_ = bf16[384,1536]{1,0:T(8,128)(2,1)S(1)} collective-permute-done((bf16[384,1536]{1,0:T(8,128)(2,1)S(1)}, bf16[384,1536]{1,0:T(8,128)(2,1)S(1)}, u32[]{:S(2)}, u32[]{:S(2)}) %collective-permute-start.41) | collective-permute-done | bytes 1179680 | tf_op jit(solution)/shard_map/ppermute | solution.py:675
  192.4 5.4 %collective-permute-done.45 = bf16[96,768]{1,0:T(8,128)(2,1)S(1)} collective-permute-done((bf16[96,768]{1,0:T(8,128)(2,1)S(1)}, bf16[96,768]{1,0:T(8,128)(2,1)S(1)}, u32[]{:S(2)}, u32[]{:S(2)}) %collective-permute-start.45) | collective-permute-done | bytes 147488 | tf_op jit(solution)/shard_map/ppermute | solution.py:675
  197.8 1.3 collective-permute-start.48
  199.1 6.7 %place.4 = f32[3072,768]{1,0:T(8,128)} custom-call(s32[2]{0:T(128)S(1)} %pad_add_fusion.here_ref, bf16[768,768]{1,0:T(8,128)(2,1)S(1)} %pad_maximum_fusion.refs_0_, bf16[768,768]{1,0:T(8,128)(2,1)S(1)} %collective-permute-done.38.refs_1_, bf16[768,768]{1,0:T(8,128)(2,1)S(1)} %collective-permute-done.43.refs_2_, ...), custom_call_target="tpu_custom_call" | custom-call | flops 1000000 | bytes 14155776 | tf_op jit(solution)/shard_map/place/pallas_call | solution.py:772
  208.6 4.9 %place.5 = f32[768,3072]{1,0:T(8,128)} custom-call(s32[2]{0:T(128)S(1)} %pad_add_fusion.here_ref, bf16[384,1536]{1,0:T(8,128)(2,1)S(1)} %pad_maximum_fusion.1.refs_0_, bf16[384,1536]{1,0:T(8,128)(2,1)S(1)} %collective-permute-done.41.refs_1_, bf16[384,1536]{1,0:T(8,128)(2,1)S(1)} %collective-permute-done.50.refs_2_, ...), custom_call_target="tpu_custom_call" | custom-call | flops 1000000 | bytes 14155776 | tf_op jit(solution)/shard_map/place/pallas_call | solution.py:772
  213.6 3.3 %collective-permute-done.49.refs_1_ = bf16[384,768]{1,0:T(8,128)(2,1)} collective-permute-done((bf16[384,768]{1,0:T(8,128)(2,1)S(1)}, bf16[384,768]{1,0:T(8,128)(2,1)}, u32[]{:S(2)}, u32[]{:S(2)}) %collective-permute-start.49) | collective-permute-done | bytes 589856 | tf_op jit(solution)/shard_map/ppermute | solution.py:675
  219.3 5.5 %place.6 = f32[768,2304]{1,0:T(8,128)} custom-call(s32[2]{0:T(128)S(1)} %pad_add_fusion.here_ref, bf16[384,1152]{1,0:T(8,128)(2,1)S(1)} %pad_maximum_fusion.2.refs_0_, bf16[384,1152]{1,0:T(8,128)(2,1)S(1)} %collective-permute-done.42.refs_1_, bf16[384,1152]{1,0:T(8,128)(2,1)S(1)} %collective-permute-done.46.refs_2_, ...), custom_call_target="tpu_custom_call" | custom-call | flops 1000000 | bytes 10616832 | tf_op jit(solution)/shard_map/place/pallas_call | solution.py:772
  224.8 5.2 %place.7 = (f32[768,768]{1,0:T(8,128)}, f32[512,768]{1,0:T(8,128)}, f32[256,768]{1,0:T(8,128)S(1)}) custom-call(s32[2]{0:T(128)S(1)} %pad_add_fusion.here_ref, bf16[384,768]{1,0:T(8,128)(2,1)S(1)} %pad_maximum_fusion.5.refs_0_, bf16[384,768]{1,0:T(8,128)(2,1)} %collective-permute-done.49.refs_1_, bf16[384,768]{1,0:T(8,128)(2,1)} %collective-permute-done.52.refs_2_, ...), custom_call_target="tpu_custom_call" | custom-call | flops 1000000 | bytes 7077888 | tf_op jit(solution)/shard_map/place/pallas_call | solution.py:772
  (126 shorter events, 21.6 us)
Async XLA Ops:
  19.2 12.6 %collective-permute-start.1 = (bf16[512,768]{1,0:T(8,128)(2,1)S(1)}, bf16[512,768]{1,0:T(8,128)(2,1)S(1)}, u32[]{:S(2)}, u32[]{:S(2)}) collective-permute-start(bf16[512,768]{1,0:T(8,128)(2,1)S(1)} %get-tuple-element.128.h2_ref.left_mine), channel_id=1, source_target_pairs={{0,16},{1,17},{2,18},{3,19},{4,20},{5,21},{6,22},{7,23},{8,24},{9,... | collective-permute-start | bytes 2359304 | tf_op jit(solution)/shard_map/ppermute | solution.py:675
  42.5 10.7 %collective-permute-start.2 = (f32[512,768]{1,0:T(8,128)S(1)}, f32[512,768]{1,0:T(8,128)S(1)}, u32[]{:S(2)}, u32[]{:S(2)}) collective-permute-start(f32[512,768]{1,0:T(8,128)S(1)} %get-tuple-element.133), channel_id=1, source_target_pairs={{0,16},{1,17},{2,18},{3,19},{4,20},{5,21},{6,22},{7,23},{8,24},{9,... | collective-permute-start | bytes 4718600 | tf_op jit(solution)/shard_map/ppermute | solution.py:675
  46.3 19.2 %collective-permute-start.4 = (bf16[768,768]{1,0:T(8,128)(2,1)S(1)}, bf16[768,768]{1,0:T(8,128)(2,1)S(1)}, u32[]{:S(2)}, u32[]{:S(2)}) collective-permute-start(bf16[768,768]{1,0:T(8,128)(2,1)S(1)} %get-tuple-element.127), channel_id=1, source_target_pairs={{0,1},{1,0},{2,3},{3,2},{4,5},{5,4},{6,7},{7,6},{8,9},{9,8},{10,11... | collective-permute-start | bytes 3538952 | tf_op jit(solution)/shard_map/ppermute | solution.py:675
  52.5 23.5 %collective-permute-start.3 = (bf16[384,1536]{1,0:T(8,128)(2,1)S(1)}, bf16[384,1536]{1,0:T(8,128)(2,1)S(1)}, u32[]{:S(2)}, u32[]{:S(2)}) collective-permute-start(bf16[384,1536]{1,0:T(8,128)(2,1)S(1)} %get-tuple-element.131), channel_id=1, source_target_pairs={{0,1},{1,0},{2,3},{3,2},{4,5},{5,4},{6,7},{7,6},{8,9},{9,8},{10,11... | collective-permute-start | bytes 3538952 | tf_op jit(solution)/shard_map/ppermute | solution.py:675
  52.6 25.7 %collective-permute-start.5 = (f32[512,768]{1,0:T(8,128)S(1)}, f32[512,768]{1,0:T(8,128)S(1)}, u32[]{:S(2)}, u32[]{:S(2)}) collective-permute-start(f32[512,768]{1,0:T(8,128)S(1)} %get-tuple-element.122), channel_id=1, source_target_pairs={{0,16},{1,17},{2,18},{3,19},{4,20},{5,21},{6,22},{7,23},{8,24},{9,... | collective-permute-start | bytes 4718600 | tf_op jit(solution)/shard_map/ppermute | solution.py:675
  52.7 36.8 %collective-permute-start.9 = (bf16[512,768]{1,0:T(8,128)(2,1)S(1)}, bf16[512,768]{1,0:T(8,128)(2,1)S(1)}, u32[]{:S(2)}, u32[]{:S(2)}) collective-permute-start(bf16[512,768]{1,0:T(8,128)(2,1)S(1)} %get-tuple-element.157.left_mine), channel_id=1, source_target_pairs={{0,16},{1,17},{2,18},{3,19},{4,20},{5,21},{6,22},{7,23},{8,24},{9,... | collective-permute-start | bytes 2359304 | tf_op jit(solution)/shard_map/ppermute | solution.py:675
  53.1 43.6 %collective-permute-start.14 = (bf16[512,768]{1,0:T(8,128)(2,1)S(1)}, bf16[512,768]{1,0:T(8,128)(2,1)S(1)}, u32[]{:S(2)}, u32[]{:S(2)}) collective-permute-start(bf16[512,768]{1,0:T(8,128)(2,1)S(1)} %get-tuple-element.162.ctx_mine), channel_id=1, source_target_pairs={{0,16},{1,17},{2,18},{3,19},{4,20},{5,21},{6,22},{7,23},{8,24},{9,... | collective-permute-start | bytes 2359304 | tf_op jit(solution)/shard_map/ppermute | solution.py:675
  65.6 24.0 %collective-permute-start.10 = (bf16[512,1152]{1,0:T(8,128)(2,1)S(1)}, bf16[512,1152]{1,0:T(8,128)(2,1)S(1)}, u32[]{:S(2)}, u32[]{:S(2)}) collective-permute-start(bf16[512,1152]{1,0:T(8,128)(2,1)S(1)} %get-tuple-element.139.gq_other), channel_id=1, source_target_pairs={{0,16},{1,17},{2,18},{3,19},{4,20},{5,21},{6,22},{7,23},{8,24},{9,... | collective-permute-start | bytes 3538952 | tf_op jit(solution)/shard_map/ppermute | solution.py:675
  76.0 13.4 %collective-permute-start.8 = (bf16[384,768]{1,0:T(8,128)(2,1)S(1)}, bf16[384,768]{1,0:T(8,128)(2,1)S(1)}, u32[]{:S(2)}, u32[]{:S(2)}) collective-permute-start(bf16[384,768]{1,0:T(8,128)(2,1)S(1)} %get-tuple-element.240), channel_id=1, source_target_pairs={{0,2},{1,3},{2,0},{3,1},{4,6},{5,7},{6,4},{7,5},{8,10},{9,11},{10,... | collective-permute-start | bytes 1769480 | tf_op jit(solution)/shard_map/ppermute | solution.py:675
  78.3 17.6 %collective-permute-start.7 = (bf16[192,1536]{1,0:T(8,128)(2,1)S(1)}, bf16[192,1536]{1,0:T(8,128)(2,1)S(1)}, u32[]{:S(2)}, u32[]{:S(2)}) collective-permute-start(bf16[192,1536]{1,0:T(8,128)(2,1)S(1)} %get-tuple-element.242), channel_id=1, source_target_pairs={{0,2},{1,3},{2,0},{3,1},{4,6},{5,7},{6,4},{7,5},{8,10},{9,11},{10,... | collective-permute-start | bytes 1769480 | tf_op jit(solution)/shard_map/ppermute | solution.py:675
  92.5 16.5 %collective-permute-start.12 = (bf16[384,1152]{1,0:T(8,128)(2,1)S(1)}, bf16[384,1152]{1,0:T(8,128)(2,1)S(1)}, u32[]{:S(2)}, u32[]{:S(2)}) collective-permute-start(bf16[384,1152]{1,0:T(8,128)(2,1)S(1)} %get-tuple-element.158), channel_id=1, source_target_pairs={{0,1},{1,0},{2,3},{3,2},{4,5},{5,4},{6,7},{7,6},{8,9},{9,8},{10,11... | collective-permute-start | bytes 2654216 | tf_op jit(solution)/shard_map/ppermute | solution.py:675
  95.9 9.9 %collective-permute-start.13 = (bf16[192,768]{1,0:T(8,128)(2,1)S(1)}, bf16[192,768]{1,0:T(8,128)(2,1)S(1)}, u32[]{:S(2)}, u32[]{:S(2)}) collective-permute-start(bf16[192,768]{1,0:T(8,128)(2,1)S(1)} %get-tuple-element.248), channel_id=1, source_target_pairs={{0,4},{1,5},{2,6},{3,7},{4,0},{5,1},{6,2},{7,3},{8,12},{9,13},{10,... | collective-permute-start | bytes 884744 | tf_op jit(solution)/shard_map/ppermute | solution.py:675
  96.7 20.8 %collective-permute-start.6 = (f32[32,768]{1,0:T(8,128)S(1)}, f32[32,768]{1,0:T(8,128)S(1)}, u32[]{:S(2)}, u32[]{:S(2)}) collective-permute-start(f32[32,768]{1,0:T(8,128)S(1)} %get-tuple-element.154), channel_id=1, source_target_pairs={{0,16},{1,17},{2,18},{3,19},{4,20},{5,21},{6,22},{7,23},{8,24},{9,... | collective-permute-start | bytes 294920 | tf_op jit(solution)/shard_map/ppermute | solution.py:675
  97.9 13.3 %collective-permute-start.11 = (bf16[96,1536]{1,0:T(8,128)(2,1)S(1)}, bf16[96,1536]{1,0:T(8,128)(2,1)S(1)}, u32[]{:S(2)}, u32[]{:S(2)}) collective-permute-start(bf16[96,1536]{1,0:T(8,128)(2,1)S(1)} %get-tuple-element.249), channel_id=1, source_target_pairs={{0,4},{1,5},{2,6},{3,7},{4,0},{5,1},{6,2},{7,3},{8,12},{9,13},{10,... | collective-permute-start | bytes 884744 | tf_op jit(solution)/shard_map/ppermute | solution.py:675
  100.4 18.4 %collective-permute-start.21 = (bf16[384,768]{1,0:T(8,128)(2,1)S(1)}, bf16[384,768]{1,0:T(8,128)(2,1)S(1)}, u32[]{:S(2)}, u32[]{:S(2)}) collective-permute-start(bf16[384,768]{1,0:T(8,128)(2,1)S(1)} %get-tuple-element.167), channel_id=1, source_target_pairs={{0,1},{1,0},{2,3},{3,2},{4,5},{5,4},{6,7},{7,6},{8,9},{9,8},{10,11... | collective-permute-start | bytes 1769480 | tf_op jit(solution)/shard_map/ppermute | solution.py:675
  105.8 11.8 %collective-permute-start.18 = (bf16[96,768]{1,0:T(8,128)(2,1)S(1)}, bf16[96,768]{1,0:T(8,128)(2,1)S(1)}, u32[]{:S(2)}, u32[]{:S(2)}) collective-permute-start(bf16[96,768]{1,0:T(8,128)(2,1)S(1)} %add_convert_fusion.21), channel_id=1, source_target_pairs={{0,12},{1,13},{2,14},{3,15},{4,8},{5,9},{6,10},{7,11},{8,4},{9,5},... | collective-permute-start | bytes 442376 | tf_op jit(solution)/shard_map/ppermute | solution.py:675
  109.3 9.1 %collective-permute-start.22 = (bf16[192,1152]{1,0:T(8,128)(2,1)S(1)}, bf16[192,1152]{1,0:T(8,128)(2,1)S(1)}, u32[]{:S(2)}, u32[]{:S(2)}) collective-permute-start(bf16[192,1152]{1,0:T(8,128)(2,1)S(1)} %get-tuple-element.244), channel_id=1, source_target_pairs={{0,2},{1,3},{2,0},{3,1},{4,6},{5,7},{6,4},{7,5},{8,10},{9,11},{10,... | collective-permute-start | bytes 1327112 | tf_op jit(solution)/shard_map/ppermute | solution.py:675
  111.3 10.0 %collective-permute-start.20 = (bf16[48,1536]{1,0:T(8,128)(2,1)S(1)}, bf16[48,1536]{1,0:T(8,128)(2,1)S(1)}, u32[]{:S(2)}, u32[]{:S(2)}) collective-permute-start(bf16[48,1536]{1,0:T(8,128)(2,1)S(1)} %add_convert_fusion.20), channel_id=1, source_target_pairs={{0,12},{1,13},{2,14},{3,15},{4,8},{5,9},{6,10},{7,11},{8,4},{9,5},... | collective-permute-start | bytes 442376 | tf_op jit(solution)/shard_map/ppermute | solution.py:675
  117.6 15.3 %collective-permute-start.17 = (f32[32,768]{1,0:T(8,128)S(1)}, f32[32,768]{1,0:T(8,128)S(1)}, u32[]{:S(2)}, u32[]{:S(2)}) collective-permute-start(f32[32,768]{1,0:T(8,128)S(1)} %add.110), channel_id=1, source_target_pairs={{0,1},{1,0},{2,3},{3,2},{4,5},{5,4},{6,7},{7,6},{8,9},{9,8},{10,11... | collective-permute-start | bytes 294920 | tf_op jit(solution)/shard_map/ppermute | solution.py:675
  117.7 8.8 %collective-permute-start.19 = (bf16[96,768]{1,0:T(8,128)(2,1)S(1)}, bf16[96,768]{1,0:T(8,128)(2,1)S(1)}, u32[]{:S(2)}, u32[]{:S(2)}) collective-permute-start(bf16[96,768]{1,0:T(8,128)(2,1)S(1)} %add_convert_fusion.18), channel_id=1, source_target_pairs={{0,12},{1,13},{2,14},{3,15},{4,8},{5,9},{6,10},{7,11},{8,4},{9,5},... | collective-permute-start | bytes 442376 | tf_op jit(solution)/shard_map/ppermute | solution.py:675
  118.5 14.5 %collective-permute-start.24 = (bf16[96,1152]{1,0:T(8,128)(2,1)S(1)}, bf16[96,1152]{1,0:T(8,128)(2,1)S(1)}, u32[]{:S(2)}, u32[]{:S(2)}) collective-permute-start(bf16[96,1152]{1,0:T(8,128)(2,1)S(1)} %get-tuple-element.252), channel_id=1, source_target_pairs={{0,4},{1,5},{2,6},{3,7},{4,0},{5,1},{6,2},{7,3},{8,12},{9,13},{10,... | collective-permute-start | bytes 663560 | tf_op jit(solution)/shard_map/ppermute | solution.py:675
  119.0 16.4 %collective-permute-start.28 = (bf16[192,768]{1,0:T(8,128)(2,1)S(1)}, bf16[192,768]{1,0:T(8,128)(2,1)S(1)}, u32[]{:S(2)}, u32[]{:S(2)}) collective-permute-start(bf16[192,768]{1,0:T(8,128)(2,1)S(1)} %get-tuple-element.246), channel_id=1, source_target_pairs={{0,2},{1,3},{2,0},{3,1},{4,6},{5,7},{6,4},{7,5},{8,10},{9,11},{10,... | collective-permute-start | bytes 884744 | tf_op jit(solution)/shard_map/ppermute | solution.py:675
  121.4 14.2 %collective-permute-start.27 = (bf16[48,1536]{1,0:T(8,128)(2,1)S(1)}, bf16[48,1536]{1,0:T(8,128)(2,1)S(1)}, u32[]{:S(2)}, u32[]{:S(2)}) collective-permute-start(bf16[48,1536]{1,0:T(8,128)(2,1)S(1)} %add_convert_fusion.16), channel_id=1, source_target_pairs={{0,12},{1,13},{2,14},{3,15},{4,8},{5,9},{6,10},{7,11},{8,4},{9,5},... | collective-permute-start | bytes 442376 | tf_op jit(solution)/shard_map/ppermute | solution.py:675
  126.5 15.5 %collective-permute-start.26 = (bf16[192,768]{1,0:T(8,128)(2,1)S(1)}, bf16[192,768]{1,0:T(8,128)(2,1)S(1)}, u32[]{:S(2)}, u32[]{:S(2)}) collective-permute-start(bf16[192,768]{1,0:T(8,128)(2,1)S(1)} %pad_maximum_fusion.7), channel_id=1, source_target_pairs={{0,4},{1,5},{2,6},{3,7},{4,0},{5,1},{6,2},{7,3},{8,12},{9,13},{10,... | collective-permute-start | bytes 884744 | tf_op jit(solution)/shard_map/ppermute | solution.py:675
  132.9 14.2 %collective-permute-start.23 = (f32[32,768]{1,0:T(8,128)S(1)}, f32[32,768]{1,0:T(8,128)S(1)}, u32[]{:S(2)}, u32[]{:S(2)}) collective-permute-start(f32[32,768]{1,0:T(8,128)S(1)} %add.118), channel_id=1, source_target_pairs={{0,2},{1,3},{2,0},{3,1},{4,6},{5,7},{6,4},{7,5},{8,10},{9,11},{10,... | collective-permute-start | bytes 294920 | tf_op jit(solution)/shard_map/ppermute | solution.py:675
  133.0 12.5 %collective-permute-start.25 = (bf16[48,1152]{1,0:T(8,128)(2,1)S(1)}, bf16[48,1152]{1,0:T(8,128)(2,1)S(1)}, u32[]{:S(2)}, u32[]{:S(2)}) collective-permute-start(bf16[48,1152]{1,0:T(8,128)(2,1)S(1)} %add_convert_fusion.23), channel_id=1, source_target_pairs={{0,12},{1,13},{2,14},{3,15},{4,8},{5,9},{6,10},{7,11},{8,4},{9,5},... | collective-permute-start | bytes 331784 | tf_op jit(solution)/shard_map/ppermute | solution.py:675
  135.5 11.7 %collective-permute-start.30 = (bf16[96,768]{1,0:T(8,128)(2,1)S(1)}, bf16[96,768]{1,0:T(8,128)(2,1)S(1)}, u32[]{:S(2)}, u32[]{:S(2)}) collective-permute-start(bf16[96,768]{1,0:T(8,128)(2,1)S(1)} %get-tuple-element.254), channel_id=1, source_target_pairs={{0,4},{1,5},{2,6},{3,7},{4,0},{5,1},{6,2},{7,3},{8,12},{9,13},{10,... | collective-permute-start | bytes 442376 | tf_op jit(solution)/shard_map/ppermute | solution.py:675
  135.6 17.4 %collective-permute-start.34 = (bf16[96,1536]{1,0:T(8,128)(2,1)S(1)}, bf16[96,1536]{1,0:T(8,128)(2,1)S(1)}, u32[]{:S(2)}, u32[]{:S(2)}) collective-permute-start(bf16[96,1536]{1,0:T(8,128)(2,1)S(1)} %pad_maximum_fusion.8), channel_id=1, source_target_pairs={{0,4},{1,5},{2,6},{3,7},{4,0},{5,1},{6,2},{7,3},{8,12},{9,13},{10,... | collective-permute-start | bytes 884744 | tf_op jit(solution)/shard_map/ppermute | solution.py:675
  142.0 11.6 %collective-permute-start.33 = (bf16[384,768]{1,0:T(8,128)(2,1)S(1)}, bf16[384,768]{1,0:T(8,128)(2,1)S(1)}, u32[]{:S(2)}, u32[]{:S(2)}) collective-permute-start(bf16[384,768]{1,0:T(8,128)(2,1)S(1)} %pad_maximum_fusion.3), channel_id=1, source_target_pairs={{0,2},{1,3},{2,0},{3,1},{4,6},{5,7},{6,4},{7,5},{8,10},{9,11},{10,... | collective-permute-start | bytes 1769480 | tf_op jit(solution)/shard_map/ppermute | solution.py:675
  145.6 10.3 %collective-permute-start.32 = (bf16[48,1152]{1,0:T(8,128)(2,1)S(1)}, bf16[48,1152]{1,0:T(8,128)(2,1)S(1)}, u32[]{:S(2)}, u32[]{:S(2)}) collective-permute-start(bf16[48,1152]{1,0:T(8,128)(2,1)S(1)} %add_convert_fusion.22), channel_id=1, source_target_pairs={{0,12},{1,13},{2,14},{3,15},{4,8},{5,9},{6,10},{7,11},{8,4},{9,5},... | collective-permute-start | bytes 331784 | tf_op jit(solution)/shard_map/ppermute | solution.py:675
  147.1 9.4 %collective-permute-start.29 = (f32[32,768]{1,0:T(8,128)S(1)}, f32[32,768]{1,0:T(8,128)S(1)}, u32[]{:S(2)}, u32[]{:S(2)}) collective-permute-start(f32[32,768]{1,0:T(8,128)S(1)} %add.125), channel_id=1, source_target_pairs={{0,4},{1,5},{2,6},{3,7},{4,0},{5,1},{6,2},{7,3},{8,12},{9,13},{10,... | collective-permute-start | bytes 294920 | tf_op jit(solution)/shard_map/ppermute | solution.py:675
  147.2 9.3 %collective-permute-start.31 = (bf16[48,768]{1,0:T(8,128)(2,1)S(1)}, bf16[48,768]{1,0:T(8,128)(2,1)S(1)}, u32[]{:S(2)}, u32[]{:S(2)}) collective-permute-start(bf16[48,768]{1,0:T(8,128)(2,1)S(1)} %add_convert_fusion.26), channel_id=1, source_target_pairs={{0,12},{1,13},{2,14},{3,15},{4,8},{5,9},{6,10},{7,11},{8,4},{9,5},... | collective-permute-start | bytes 221192 | tf_op jit(solution)/shard_map/ppermute | solution.py:675
  153.1 16.3 %collective-permute-start.39 = (bf16[192,1536]{1,0:T(8,128)(2,1)S(1)}, bf16[192,1536]{1,0:T(8,128)(2,1)S(1)}, u32[]{:S(2)}, u32[]{:S(2)}) collective-permute-start(bf16[192,1536]{1,0:T(8,128)(2,1)S(1)} %pad_maximum_fusion.4), channel_id=1, source_target_pairs={{0,2},{1,3},{2,0},{3,1},{4,6},{5,7},{6,4},{7,5},{8,10},{9,11},{10,... | collective-permute-start | bytes 1769480 | tf_op jit(solution)/shard_map/ppermute | solution.py:675
  153.7 18.8 %collective-permute-start.38 = (bf16[768,768]{1,0:T(8,128)(2,1)S(1)}, bf16[768,768]{1,0:T(8,128)(2,1)S(1)}, u32[]{:S(2)}, u32[]{:S(2)}) collective-permute-start(bf16[768,768]{1,0:T(8,128)(2,1)S(1)} %pad_maximum_fusion.refs_0_), channel_id=1, source_target_pairs={{0,1},{1,0},{2,3},{3,2},{4,5},{5,4},{6,7},{7,6},{8,9},{9,8},{10,11... | collective-permute-start | bytes 3538952 | tf_op jit(solution)/shard_map/ppermute | solution.py:675
  169.5 21.0 %collective-permute-start.41 = (bf16[384,1536]{1,0:T(8,128)(2,1)S(1)}, bf16[384,1536]{1,0:T(8,128)(2,1)S(1)}, u32[]{:S(2)}, u32[]{:S(2)}) collective-permute-start(bf16[384,1536]{1,0:T(8,128)(2,1)S(1)} %pad_maximum_fusion.1.refs_0_), channel_id=1, source_target_pairs={{0,1},{1,0},{2,3},{3,2},{4,5},{5,4},{6,7},{7,6},{8,9},{9,8},{10,11... | collective-permute-start | bytes 3538952 | tf_op jit(solution)/shard_map/ppermute | solution.py:675
  176.0 14.5 %collective-permute-start.40 = (bf16[192,1152]{1,0:T(8,128)(2,1)S(1)}, bf16[192,1152]{1,0:T(8,128)(2,1)S(1)}, u32[]{:S(2)}, u32[]{:S(2)}) collective-permute-start(bf16[192,1152]{1,0:T(8,128)(2,1)S(1)} %pad_maximum_fusion.6), channel_id=1, source_target_pairs={{0,2},{1,3},{2,0},{3,1},{4,6},{5,7},{6,4},{7,5},{8,10},{9,11},{10,... | collective-permute-start | bytes 1327112 | tf_op jit(solution)/shard_map/ppermute | solution.py:675
  178.1 19.7 %collective-permute-start.43 = (bf16[768,768]{1,0:T(8,128)(2,1)S(1)}, bf16[768,768]{1,0:T(8,128)(2,1)S(1)}, u32[]{:S(2)}, u32[]{:S(2)}) collective-permute-start(bf16[768,768]{1,0:T(8,128)(2,1)S(1)} %pad_maximum_fusion.refs_0_), channel_id=1, source_target_pairs={{0,16},{1,17},{2,18},{3,19},{4,20},{5,21},{6,22},{7,23},{8,24},{9,... | collective-permute-start | bytes 3538952 | tf_op jit(solution)/shard_map/ppermute | solution.py:675
  179.4 7.4 %collective-permute-start.35 = (f32[32,768]{1,0:T(8,128)S(1)}, f32[32,768]{1,0:T(8,128)S(1)}, u32[]{:S(2)}, u32[]{:S(2)}) collective-permute-start(f32[32,768]{1,0:T(8,128)S(1)} %add.130), channel_id=1, source_target_pairs={{0,12},{1,13},{2,14},{3,15},{4,8},{5,9},{6,10},{7,11},{8,4},{9,5},... | collective-permute-start | bytes 294920 | tf_op jit(solution)/shard_map/ppermute | solution.py:675
  185.1 14.0 %collective-permute-start.44 = (bf16[768,768]{1,0:T(8,128)(2,1)S(1)}, bf16[768,768]{1,0:T(8,128)(2,1)S(1)}, u32[]{:S(2)}, u32[]{:S(2)}) collective-permute-start(bf16[768,768]{1,0:T(8,128)(2,1)S(1)} %collective-permute-done.38.refs_1_), channel_id=1, source_target_pairs={{0,16},{1,17},{2,18},{3,19},{4,20},{5,21},{6,22},{7,23},{8,24},{9,... | collective-permute-start | bytes 3538952 | tf_op jit(solution)/shard_map/ppermute | solution.py:675
  190.6 15.8 %collective-permute-start.42 = (bf16[384,1152]{1,0:T(8,128)(2,1)S(1)}, bf16[384,1152]{1,0:T(8,128)(2,1)S(1)}, u32[]{:S(2)}, u32[]{:S(2)}) collective-permute-start(bf16[384,1152]{1,0:T(8,128)(2,1)S(1)} %pad_maximum_fusion.2.refs_0_), channel_id=1, source_target_pairs={{0,1},{1,0},{2,3},{3,2},{4,5},{5,4},{6,7},{7,6},{8,9},{9,8},{10,11... | collective-permute-start | bytes 2654216 | tf_op jit(solution)/shard_map/ppermute | solution.py:675
  192.4 15.8 %collective-permute-start.50 = (bf16[384,1536]{1,0:T(8,128)(2,1)S(1)}, bf16[384,1536]{1,0:T(8,128)(2,1)S(1)}, u32[]{:S(2)}, u32[]{:S(2)}) collective-permute-start(bf16[384,1536]{1,0:T(8,128)(2,1)S(1)} %pad_maximum_fusion.1.refs_0_), channel_id=1, source_target_pairs={{0,16},{1,17},{2,18},{3,19},{4,20},{5,21},{6,22},{7,23},{8,24},{9,... | collective-permute-start | bytes 3538952 | tf_op jit(solution)/shard_map/ppermute | solution.py:675
  197.8 10.9 %collective-permute-start.51 = (bf16[384,1536]{1,0:T(8,128)(2,1)S(1)}, bf16[384,1536]{1,0:T(8,128)(2,1)S(1)}, u32[]{:S(2)}, u32[]{:S(2)}) collective-permute-start(bf16[384,1536]{1,0:T(8,128)(2,1)S(1)} %collective-permute-done.41.refs_1_), channel_id=1, source_target_pairs={{0,16},{1,17},{2,18},{3,19},{4,20},{5,21},{6,22},{7,23},{8,24},{9,... | collective-permute-start | bytes 3538952 | tf_op jit(solution)/shard_map/ppermute | solution.py:675
  197.8 8.9 %collective-permute-start.48 = (bf16[192,768]{1,0:T(8,128)(2,1)S(1)}, bf16[192,768]{1,0:T(8,128)(2,1)S(1)}, u32[]{:S(2)}, u32[]{:S(2)}) collective-permute-start(bf16[192,768]{1,0:T(8,128)(2,1)S(1)} %pad_maximum_fusion.9), channel_id=1, source_target_pairs={{0,2},{1,3},{2,0},{3,1},{4,6},{5,7},{6,4},{7,5},{8,10},{9,11},{10,... | collective-permute-start | bytes 884744 | tf_op jit(solution)/shard_map/ppermute | solution.py:675
  206.8 10.1 %collective-permute-start.49 = (bf16[384,768]{1,0:T(8,128)(2,1)S(1)}, bf16[384,768]{1,0:T(8,128)(2,1)}, u32[]{:S(2)}, u32[]{:S(2)}) collective-permute-start(bf16[384,768]{1,0:T(8,128)(2,1)S(1)} %pad_maximum_fusion.5.refs_0_), channel_id=1, source_target_pairs={{0,1},{1,0},{2,3},{3,2},{4,5},{5,4},{6,7},{7,6},{8,9},{9,8},{10,11... | collective-permute-start | bytes 1769480 | tf_op jit(solution)/shard_map/ppermute | solution.py:675
  207.5 11.8 %collective-permute-start.46 = (bf16[384,1152]{1,0:T(8,128)(2,1)S(1)}, bf16[384,1152]{1,0:T(8,128)(2,1)S(1)}, u32[]{:S(2)}, u32[]{:S(2)}) collective-permute-start(bf16[384,1152]{1,0:T(8,128)(2,1)S(1)} %pad_maximum_fusion.2.refs_0_), channel_id=1, source_target_pairs={{0,16},{1,17},{2,18},{3,19},{4,20},{5,21},{6,22},{7,23},{8,24},{9,... | collective-permute-start | bytes 2654216 | tf_op jit(solution)/shard_map/ppermute | solution.py:675
  208.1 11.2 %collective-permute-start.47 = (bf16[384,1152]{1,0:T(8,128)(2,1)S(1)}, bf16[384,1152]{1,0:T(8,128)(2,1)}, u32[]{:S(2)}, u32[]{:S(2)}) collective-permute-start(bf16[384,1152]{1,0:T(8,128)(2,1)S(1)} %collective-permute-done.42.refs_1_), channel_id=1, source_target_pairs={{0,16},{1,17},{2,18},{3,19},{4,20},{5,21},{6,22},{7,23},{8,24},{9,... | collective-permute-start | bytes 2654216 | tf_op jit(solution)/shard_map/ppermute | solution.py:675
  208.1 16.7 %collective-permute-start.52 = (bf16[384,768]{1,0:T(8,128)(2,1)S(1)}, bf16[384,768]{1,0:T(8,128)(2,1)}, u32[]{:S(2)}, u32[]{:S(2)}) collective-permute-start(bf16[384,768]{1,0:T(8,128)(2,1)S(1)} %pad_maximum_fusion.5.refs_0_), channel_id=1, source_target_pairs={{0,16},{1,17},{2,18},{3,19},{4,20},{5,21},{6,22},{7,23},{8,24},{9,... | collective-permute-start | bytes 1769480 | tf_op jit(solution)/shard_map/ppermute | solution.py:675
  216.8 8.0 %collective-permute-start.53 = (bf16[384,768]{1,0:T(8,128)(2,1)}, bf16[384,768]{1,0:T(8,128)(2,1)}, u32[]{:S(2)}, u32[]{:S(2)}) collective-permute-start(bf16[384,768]{1,0:T(8,128)(2,1)} %collective-permute-done.49.refs_1_), channel_id=1, source_target_pairs={{0,16},{1,17},{2,18},{3,19},{4,20},{5,21},{6,22},{7,23},{8,24},{9,... | collective-permute-start | bytes 1769480 | tf_op jit(solution)/shard_map/ppermute | solution.py:675
  (11 other events, 75.5 us)
